TPU v7x, 128 devices: a whole 4x4x4 slice. The times are simulated.
128 devices in a mesh: dp: 32 (over z, x_hi, y), blk: 4 (over x_lo, core).
Axes of the slice: x: 4 (x_hi: 2, x_lo: 2; x = x_hi * 2 + x_lo), y: 4, z: 4, core: 2. Of those that a mesh axis runs over, the one named last changes fastest.
Arguments:
- queries: bfloat16 [32768, 4096], P(('dp', 'blk')), may hold values from -24 to 24
- passages: bfloat16 [32768, 4096], P(('dp', 'blk')), may hold values from -16 to 16
- hard_owner: int32 [32768, 1], P(('dp', 'blk')), may hold values from 0 to 31, as said below
- hard_row: int32 [32768, 1], P(('dp', 'blk')), may hold values from 0 to 255
Outputs:
- query_embedding_gradient: float32 [32768, 4096], P(('dp', 'blk'))
- passage_grad: float32 [32768, 4096], P(('dp', 'blk'))
- loss: float32 [], replicated
Inputs may be any that keep to these rules, and one draw needn't show every extreme that they name: `hard_owner`: the rows of one device name no owner more than 10 times, and one owner exactly 10 times.
All inputs are finite; a program needn't handle non-finite values.
Results may differ from a plain program's by a relative error of at most 0.0025.
Values may be sent and summed in bfloat16 or wider, within the bound.
No kernel may reach another device: no remote copies, remote signals or barrier semaphores. Data moves between devices by JAX's collectives and lax.ppermute only.
A program may use at most 128 MiB of HBM per device.

v0:
```python
import math

import jax
import jax.numpy as jnp
from jax import lax
from jax.sharding import PartitionSpec as P

HARD = 1


def shards(queries, passages, hard_owner, hard_row):
    rows_dev, coordinate_count = queries.shape
    cycle_size = lax.axis_size("blk")
    shard_count = lax.axis_size("dp")
    blk_index = lax.axis_index("blk")
    logit_sharpness_factor = 2.0 / math.sqrt(coordinate_count)
    slot_count = max(2, rows_dev * HARD * 5 // (4 * shard_count))
    all_pass = lax.all_gather(passages, "blk", axis=0, tiled=True)
    similarity_logits_within = (
        jnp.einsum("bd,cd->bc", queries, all_pass, preferred_element_type=jnp.float32)
        * logit_sharpness_factor
    )
    flat_owner = hard_owner.reshape(-1)
    flat_row = hard_row.reshape(-1)
    owner_hits = (flat_owner[:, None] == jnp.arange(shard_count, dtype=jnp.int32)[None, :]).astype(
        jnp.int32
    )
    earlier = jnp.cumsum(owner_hits, axis=0) - owner_hits
    slot_index = jnp.sum(earlier * owner_hits, axis=1)
    slot_place = flat_owner * slot_count + slot_index
    requests = jnp.zeros((shard_count * slot_count,), jnp.int32).at[slot_place].set(flat_row)
    requests = requests.reshape(shard_count, slot_count)
    asked_rows = lax.all_to_all(requests, "dp", split_axis=0, concat_axis=0, tiled=True)
    picked = jnp.take(passages, asked_rows, axis=0)
    replies = lax.all_to_all(picked, "dp", split_axis=0, concat_axis=0, tiled=True)
    fetched, asked_rows = (replies, asked_rows)
    distractor_latent_matrix = fetched.reshape(shard_count * slot_count, coordinate_count)[
        slot_place
    ]
    distractor_latent_matrix = distractor_latent_matrix.reshape(rows_dev, HARD, coordinate_count)
    distractor_similarity_logits = (
        jnp.einsum(
            "sl,srl->sr", queries, distractor_latent_matrix, preferred_element_type=jnp.float32
        )
        * logit_sharpness_factor
    )
    row_top = jnp.maximum(
        jnp.max(similarity_logits_within, axis=1), jnp.max(distractor_similarity_logits, axis=1)
    )
    row_total = jnp.sum(jnp.exp(similarity_logits_within - row_top[:, None]), axis=1) + jnp.sum(
        jnp.exp(distractor_similarity_logits - row_top[:, None]), axis=1
    )
    log_norm = row_top + jnp.log(row_total)
    own_column = blk_index * rows_dev + jnp.arange(rows_dev, dtype=jnp.int32)
    positive = jnp.take_along_axis(similarity_logits_within, own_column[:, None], axis=1)[:, 0]
    loss_total = lax.psum(jnp.sum(log_norm - positive), ("dp", "blk"))
    loss = loss_total / (rows_dev * cycle_size * shard_count)
    is_positive = (
        jnp.arange(cycle_size * rows_dev, dtype=jnp.int32)[None, :] == own_column[:, None]
    ).astype(jnp.float32)
    inbatch_weights = (jnp.exp(similarity_logits_within - log_norm[:, None]) - is_positive).astype(
        jnp.bfloat16
    )
    mined_negative_weights = jnp.exp(distractor_similarity_logits - log_norm[:, None]).astype(
        jnp.bfloat16
    )
    query_embedding_gradient = jnp.dot(
        inbatch_weights, all_pass, preferred_element_type=jnp.float32
    ) + jnp.einsum(
        "ro,roc->rc",
        mined_negative_weights,
        distractor_latent_matrix,
        preferred_element_type=jnp.float32,
    )
    hard_terms = mined_negative_weights[:, :, None] * queries[:, None, :]
    outgoing = (
        jnp.zeros((shard_count * slot_count, coordinate_count), jnp.bfloat16)
        .at[slot_place]
        .set(hard_terms.reshape(-1, coordinate_count))
    )
    outgoing = outgoing.reshape(shard_count, slot_count, coordinate_count)
    got_terms = lax.all_to_all(outgoing, "dp", split_axis=0, concat_axis=0, tiled=True)
    row_hits = (
        asked_rows.reshape(-1)[None, :] == jnp.arange(rows_dev, dtype=jnp.int32)[:, None]
    ).astype(jnp.bfloat16)
    hard_part = jnp.dot(
        row_hits, got_terms.reshape(-1, coordinate_count), preferred_element_type=jnp.float32
    )
    in_part = lax.psum_scatter(
        jnp.einsum("bc,bd->cd", inbatch_weights, queries, preferred_element_type=jnp.float32),
        "blk",
        scatter_dimension=0,
        tiled=True,
    )
    passage_grad = in_part + hard_part
    return (query_embedding_gradient, passage_grad, loss)


def solution(mesh):
    return jax.shard_map(
        shards,
        mesh=mesh,
        in_specs=(
            P(("dp", "blk"), None),
            P(("dp", "blk"), None),
            P(("dp", "blk"), None),
            P(("dp", "blk"), None),
        ),
        out_specs=(P(("dp", "blk"), None), P(("dp", "blk"), None), P()),
        check_vma=False,
    )
```

profile of v0, /device:TPU:4, one launch (start us, length us, event | category | flops | bytes accessed | tf_op | source)
XLA Modules:
  0.0 378.5 jit_solution(6425774671623922384)
XLA Ops:
  7.9 0.7 fusion.9
  9.4 0.8 fusion.8
  10.9 1.6 scatter_custom_fusion
  12.5 17.9 %all_to_all.25 = s32[32,1,10]{2,1,0:T(1,128)S(1)} all-to-all(s32[32,1,10]{2,1,0:T(1,128)S(1)} %bitcast.40), channel_id=1, replica_groups=mesh['dp'=32,'blk'=4] {'dp'}, dimensions={0} | all-to-all | bytes 2560 | tf_op jit(solution)/shard_map/all_to_all | solution.py:33
  30.6 3.9 %gather_fusion = bf16[320,4096]{1,0:T(8,128)(2,1)} fusion(bf16[256,4096]{1,0:T(8,128)(2,1)S(1)} %copy-done, s32[1024]{0:T(1024)S(1)} %pad_clamp_fusion.1), kind=kCustom, calls=%fused_computation | custom fusion | bytes 5244160 | tf_op jit(solution)/shard_map/jit(_take)/gather | solution.py:34
  34.4 4.6 %reshape.154 = bf16[32,10,4096]{2,1,0:T(8,128)(2,1)} reshape(bf16[320,4096]{1,0:T(8,128)(2,1)} %gather_fusion) | data formatting | bytes 5242880 | tf_op jit(solution)/shard_map/jit(_take)/gather | solution.py:34
  39.1 4.6 %broadcast_select_fusion = bf16[32,10,4096]{2,1,0:T(8,128)(2,1)} fusion(bf16[32,10,4096]{2,1,0:T(8,128)(2,1)} %reshape.154, pred[32,10]{1,0:T(8,128)(4,1)S(1)} %compare_and_fusion), kind=kLoop, calls=%fused_computation.10 | loop fusion | flops 1310720 | bytes 5243200 | tf_op jit(solution)/shard_map/jit(_take)/select_n | solution.py:34
  43.7 7.5 %all-to-all-start.1 = ((bf16[32,10,4096]{2,1,0:T(8,128)(2,1)}), bf16[32,10,4096]{2,1,0:T(8,128)(2,1)}, u32[]{:S(2)}, u32[]{:S(2)}) async-start(bf16[32,10,4096]{2,1,0:T(8,128)(2,1)} %broadcast_select_fusion), calls=%async_computation.1 | async-start | bytes 8388608 | tf_op jit(solution)/shard_map/all_to_all | solution.py:35
  51.6 87.1 %all-to-all-done.1 = bf16[32,10,4096]{2,1,0:T(8,128)(2,1)} async-done(((bf16[32,10,4096]{2,1,0:T(8,128)(2,1)}), bf16[32,10,4096]{2,1,0:T(8,128)(2,1)}, u32[]{:S(2)}, u32[]{:S(2)}) %all-to-all-start.1) | async-done | bytes 2621472 | tf_op jit(solution)/shard_map/all_to_all | solution.py:35
  138.7 3.3 reshape.150
  142.0 3.2 gather_fusion.1
  145.2 3.0 fusion
  148.2 6.7 %fusion.19 = (f32[256]{0:T(256)S(1)}, f32[256,1024]{1,0:T(8,128)}) fusion(bf16[256,4096]{1,0:T(8,128)(2,1)S(1)} %copy-done.1, bf16[1024,4096]{1,0:T(8,128)(2,1)} %all-gather.2.cloned.1.call-done), kind=kOutput, calls=%fused_computation.55 | convolution fusion | flops 2148007680 | bytes 11535360 | tf_op jit(solution)/shard_map/bd,cd->bc/dot_general | solution.py:20
  154.9 4.4 %gather_fusion.2 = f32[256]{0:T(256)S(1)} fusion(f32[256,1024]{1,0:T(8,128)} %get-tuple-element.8, s32[256]{0:T(256)S(1)} %bitcast.37), kind=kCustom, calls=%fused_computation.2 | custom fusion | bytes 4096 | tf_op jit(solution)/shard_map/jit(take_along_axis)/gather | solution.py:55
  159.4 1.5 exponential_reduce_fusion
  161.5 9.5 %fusion.17 = f32[1024,4096]{1,0:T(8,128)} fusion(bf16[256,4096]{1,0:T(8,128)(2,1)S(1)} %copy-done.1, f32[256,1024]{1,0:T(8,128)} %get-tuple-element.8, s32[256]{0:T(256)S(1)} %iota_add_fusion, f32[256]{0:T(256)S(1)} %get-tuple-element.4), kind=kOutput, calls=%fused_computation.53 | convolution fusion | flops 2148794368 | bytes 19924992 | tf_op jit(solution)/shard_map/bc,bd->cd/dot_general | solution.py:90
  171.0 5.3 %scatter_custom_fusion.1 = bf16[320,4096]{1,0:T(8,128)(2,1)} fusion(s32[256]{0:T(256)S(1)} %bitcast.45, bf16[256,4096]{1,0:T(8,128)(2,1)S(1)} %copy-done.1, bf16[]{:T(256)} %constant.54.clone.1, bf16[256]{0:T(256)(128)(2,1)S(1)} %get-tuple-element.6), kind=kCustom, calls=%fused_computation.11 | custom fusion | flops 1048576 | bytes 4719106 | tf_op jit(solution)/shard_map/scatter | solution.py:79
  176.3 4.6 %reshape.151 = bf16[32,10,4096]{2,1,0:T(8,128)(2,1)} reshape(bf16[320,4096]{1,0:T(8,128)(2,1)} %scatter_custom_fusion.1) | data formatting | bytes 5242880 | tf_op jit(solution)/shard_map/reshape | solution.py:81
  180.9 10.3 %all-to-all-start.2 = ((bf16[32,10,4096]{2,1,0:T(8,128)(2,1)}), bf16[32,10,4096]{2,1,0:T(8,128)(2,1)}, u32[]{:S(2)}, u32[]{:S(2)}) async-start(bf16[32,10,4096]{2,1,0:T(8,128)(2,1)} %reshape.151), calls=%async_computation.3 | async-start | bytes 8388608 | tf_op jit(solution)/shard_map/all_to_all | solution.py:82
  192.5 147.6 %psum.7 = f32[]{:T(128)} all-reduce(f32[]{:T(128)} %get-tuple-element.3), channel_id=1, replica_groups=mesh['dp'=32,'blk'=4] {'dp','blk'}, use_global_device_ids=true, to_apply=%region_9.10 | all-reduce | flops 1 | bytes 8 | tf_op jit(solution)/shard_map/psum | solution.py:56
  340.8 7.9 %convolution_add_fusion.1 = f32[256,4096]{1,0:T(8,128)} fusion(bf16[1024,4096]{1,0:T(8,128)(2,1)} %all-gather.2.cloned.1.call-done, bf16[256,4096]{1,0:T(8,128)(2,1)S(1)} %copy-done.3, f32[256]{0:T(256)S(1)} %get-tuple-element.5, f32[256,1024]{1,0:T(8,128)S(1)} %copy-done.2, s32[256]{0:T(256)S(1)} %iota_add_fusion, f32[256]{0:T(256)S(1)} %get-tuple-element.4), kind=kOutput, calls=%fused_computation.8 | convolution fusion | flops 2151940096 | bytes 15731712 | tf_op jit(solution)/shard_map/dot_general | solution.py:67
  348.7 3.3 reshape.152
  352.1 13.0 %reduce-scatter.2.cloned.1.call-done = f32[256,4096]{1,0:T(8,128)} async-done(((f32[1024,4096]{1,0:T(8,128)}), f32[256,4096]{1,0:T(8,128)}) %reduce-scatter.2.cloned.1.call-update) | async-done | bytes 4194320 | tf_op jit(solution)/shard_map/reduce_scatter | solution.py:89
  365.1 5.5 %convolution_add_fusion = f32[256,4096]{1,0:T(8,128)} fusion(f32[256,4096]{1,0:T(8,128)} %reduce-scatter.2.cloned.1.call-done, bf16[320,4096]{1,0:T(8,128)(2,1)S(1)} %reshape.152, s32[320]{0:T(512)S(1)} %eq.64), kind=kOutput, calls=%fused_computation.5 | convolution fusion | flops 672219136 | bytes 11011328 | tf_op jit(solution)/shard_map/dot_general | solution.py:86
  (36 shorter events, 4.7 us)
Async XLA Ops:
  7.2 23.4 %copy-start = (bf16[256,4096]{1,0:T(8,128)(2,1)S(1)}, bf16[256,4096]{1,0:T(8,128)(2,1)}, u32[]{:S(2)}) copy-start(bf16[256,4096]{1,0:T(8,128)(2,1)} %param.5) | copy-start | bytes 6291460
  7.2 141.0 %all-gather.2.cloned.1.call-start = ((), (), s32[]{:S(2)}) async-start(), calls=%async_computation.4 | async-start | bytes 10485760 | tf_op jit(solution)/shard_map/all_gather | solution.py:18
  43.7 95.0 %all-to-all-start.1 = ((bf16[32,10,4096]{2,1,0:T(8,128)(2,1)}), bf16[32,10,4096]{2,1,0:T(8,128)(2,1)}, u32[]{:S(2)}, u32[]{:S(2)}) async-start(bf16[32,10,4096]{2,1,0:T(8,128)(2,1)} %broadcast_select_fusion), calls=%async_computation.1 | async-start | bytes 8388608 | tf_op jit(solution)/shard_map/all_to_all | solution.py:35
  51.3 313.8 %reduce-scatter.2.cloned.1.call-start = ((), (), s32[]{:S(2)}) async-start(), calls=%async_computation.5 | async-start | bytes 20971520 | tf_op jit(solution)/shard_map/reduce_scatter | solution.py:89
  145.2 3.0 copy-start.1
  180.9 159.9 %copy-start.2 = (f32[256,1024]{1,0:T(8,128)S(1)}, f32[256,1024]{1,0:T(8,128)}, u32[]{:S(2)}) copy-start(f32[256,1024]{1,0:T(8,128)} %get-tuple-element.8) | copy-start | bytes 3145732
  180.9 160.0 %copy-start.3 = (bf16[256,4096]{1,0:T(8,128)(2,1)S(1)}, bf16[256,4096]{1,0:T(8,128)(2,1)}, u32[]{:S(2)}) copy-start(bf16[256,4096]{1,0:T(8,128)(2,1)} %gather_fusion.1) | copy-start | bytes 6291460
  180.9 167.9 %all-to-all-start.2 = ((bf16[32,10,4096]{2,1,0:T(8,128)(2,1)}), bf16[32,10,4096]{2,1,0:T(8,128)(2,1)}, u32[]{:S(2)}, u32[]{:S(2)}) async-start(bf16[32,10,4096]{2,1,0:T(8,128)(2,1)} %reshape.151), calls=%async_computation.3 | async-start | bytes 8388608 | tf_op jit(solution)/shard_map/all_to_all | solution.py:82
Sparse Core Ops, SparseCore 0:
  9.7 124.7 all-gather.1
  171.1 193.9 reduce-scatter.1
where the time goes:
time: 381 us; the launch traced here: 379 us
  blocking collectives  166 us (44%)
  waiting for transfers between devices  101 us (27%)
  local copies, waits for them, and re-layouts  29.9 us (8%)
  matrix products  29.6 us (8%)
  other arithmetic  18.6 us (5%)
  starting transfers between devices  18.1 us (5%)
  between operations  16 us (4%)
    psum x1, blocking collectives, shards(): loss_total = lax.psum(jnp.sum(log_norm - positive), ('dp', 'blk'))  148 us
    all_to_all x1, waiting for transfers between devices, shards(): lax.all_to_all(picked, 'dp', split_axis=0, concat_axis=0, tiled=True)  87.1 us
    all_to_all x1, blocking collectives, shards(): lax.all_to_all(requests, 'dp', split_axis=0, concat_axis=0, tiled=True)  17.9 us
    reduce_scatter x1, waiting for transfers between devices, shards(): lax.psum_scatter(jnp.einsum('bc,bd->cd', inbatch_weights, queries, prefer...  13 us
    all_to_all x1, starting transfers between devices, shards(): lax.all_to_all(outgoing, 'dp', split_axis=0, concat_axis=0, tiled=True)  10.3 us
    dot_general x1, matrix products, shards(): jnp.einsum('bc,bd->cd', inbatch_weights, queries, preferred_element_type=...  9.47 us
    gather x2, local copies, waits for them, and re-layouts, shards(): picked = jnp.take(passages, asked_rows, axis=0)  8.45 us
    dot_general x1, matrix products, shards(): jnp.dot(inbatch_weights, all_pass, preferred_element_type=jnp.float32)  7.89 us
  transfers between devices with their start and end apart: 4, of which 2 were waited for; matrix products, arithmetic and copies ran while one was open for 13% of the time, Pallas kernels for 0%

commit v1 on v0

v1 whole, which is shorter than its diff:
```python
import functools
import math

import jax
import jax.numpy as jnp
from jax import lax
from jax.experimental import pallas as pl
from jax.experimental.pallas import tpu as pltpu
from jax.sharding import PartitionSpec as P

CAP = 10
PARTS = 4
F32, BF16 = jnp.float32, jnp.bfloat16
VMEM_BYTES = 58 * 1024 * 1024
PAIR = [(i, i ^ 2) for i in range(4)]
CORE = [(i, i ^ 1) for i in range(4)]
DIAG = [(i, i ^ 3) for i in range(4)]


def neighbour_groups():
    groups = []
    for a in range(2):
        for core in range(2):
            groups.append([m * 4 + (a ^ ((m // 4) % 2)) * 2 + core for m in range(32)])
    return groups


def dot(a, b):
    return jnp.dot(a, b, preferred_element_type=F32)


def dot_t(a, b):
    return lax.dot_general(a, b, (((1,), (1,)), ((), ())), preferred_element_type=F32)


def iota(shape, dim):
    return lax.broadcasted_iota(jnp.int32, shape, dim)


def params(**kw):
    return pltpu.CompilerParams(vmem_limit_bytes=VMEM_BYTES, **kw)


def whole(shape):
    return pl.BlockSpec(shape, lambda *_: (0,) * len(shape))


def serve_kernel(half_ref, code_ref, src_ref, *refs):
    out_ref = refs[-1]
    rows, width = src_ref.shape
    part = width // PARTS
    lane = iota((code_ref.shape[0], rows), 1)
    code = code_ref[...]
    acc = jnp.zeros(out_ref.shape, F32)
    for k in range(PARTS):
        hit = jnp.where(code == lane + rows * k, 1.0, 0.0).astype(BF16)
        acc += dot(hit, src_ref[:, k * part : (k + 1) * part])
    out_ref[...] = acc.astype(BF16)


def serve(half, codes, src, before=None):
    rows, width = src.shape
    n = codes.shape[0]
    tile = n // 8
    part = width // PARTS

    def at(i, half_ref):
        return (2 * i + half_ref[0], 0)

    extra = [] if before is None else [before]
    return pl.pallas_call(
        serve_kernel,
        grid_spec=pltpu.PrefetchScalarGridSpec(
            num_scalar_prefetch=1,
            grid=(4,),
            in_specs=[pl.BlockSpec((tile, 1), at), whole((rows, width))]
            + [pl.BlockSpec(memory_space=pl.ANY)] * len(extra),
            out_specs=pl.BlockSpec((tile, part), at),
        ),
        out_shape=jax.ShapeDtypeStruct((n, part), BF16),
        input_output_aliases={3: 0} if extra else {},
        compiler_params=params(),
        cost_estimate=pl.CostEstimate(
            flops=n * rows * width, bytes_accessed=4 * rows * width, transcendentals=0
        ),
        name="serve",
    )(half, codes, src, *extra)


def pack_kernel(place_ref, q_ref, out_ref):
    rows, width = q_ref.shape
    tile, part = out_ref.shape
    row = pl.program_id(0) * tile + iota((tile, rows), 0)
    acc = jnp.zeros((tile, part), F32)
    for k in range(PARTS):
        hit = jnp.where(row == place_ref[...] + CAP * k, 1.0, 0.0).astype(BF16)
        acc += dot(hit, q_ref[:, k * part : (k + 1) * part])
    out_ref[...] = acc.astype(BF16)


def pack(place_row, q, n):
    rows, width = q.shape
    tile = n // 8
    part = width // PARTS
    return pl.pallas_call(
        pack_kernel,
        grid=(8,),
        in_specs=[whole((1, rows)), whole((rows, width))],
        out_specs=pl.BlockSpec((tile, part), lambda i: (i, 0)),
        out_shape=jax.ShapeDtypeStruct((n, part), BF16),
        compiler_params=params(),
        cost_estimate=pl.CostEstimate(
            flops=2 * n * rows * width, bytes_accessed=4 * rows * width, transcendentals=0
        ),
        name="pack",
    )(place_row, q)


def scores_kernel(scale, q_ref, p0, p1, p2, p3, s_ref, stat_ref):
    rows = q_ref.shape[0]
    blocks = [dot_t(q_ref[...], p[...]) * scale for p in (p0, p1, p2, p3)]
    top = jnp.max(blocks[0], axis=1, keepdims=True)
    for b in blocks[1:]:
        top = jnp.maximum(top, jnp.max(b, axis=1, keepdims=True))
    total = jnp.zeros_like(top)
    for j, b in enumerate(blocks):
        total += jnp.sum(jnp.exp(b - top), axis=1, keepdims=True)
        s_ref[:, j * rows : (j + 1) * rows] = b
    eye = iota((rows, rows), 0) == iota((rows, rows), 1)
    diag = jnp.sum(jnp.where(eye, blocks[0], 0.0), axis=1, keepdims=True)
    lane = iota(stat_ref.shape, 1)
    stat_ref[...] = jnp.where(lane == 0, top, jnp.where(lane == 1, total, diag))


def scores(scale, q, passages):
    rows, width = q.shape
    full = whole((rows, width))
    return pl.pallas_call(
        functools.partial(scores_kernel, scale),
        grid=(1,),
        in_specs=[full] * 5,
        out_specs=[whole((rows, 4 * rows)), whole((rows, 128))],
        out_shape=[
            jax.ShapeDtypeStruct((rows, 4 * rows), F32),
            jax.ShapeDtypeStruct((rows, 128), F32),
        ],
        compiler_params=params(),
        cost_estimate=pl.CostEstimate(
            flops=8 * rows * rows * width,
            bytes_accessed=10 * rows * width,
            transcendentals=4 * rows * rows,
        ),
        name="scores",
    )(q, *passages)


def unpack_kernel(got_ref, place_ref, q_ref, f_ref, hard_ref):
    k = pl.program_id(0)
    rows = q_ref.shape[0]

    @pl.when(k == 0)
    def _():
        hard_ref[...] = jnp.zeros_like(hard_ref)

    lane = iota((rows, got_ref.shape[0]), 1)
    hit = jnp.where(lane == place_ref[...] + CAP * k, 1.0, 0.0).astype(BF16)
    fetched = dot(hit, got_ref[...])
    f_ref[...] = fetched.astype(BF16)
    hard_ref[...] += jnp.sum(fetched * q_ref[...].astype(F32), axis=1, keepdims=True)


def unpack(got, place_col, q):
    rows = q.shape[0]
    n, part = got.shape
    col = pl.BlockSpec((rows, part), lambda k: (0, k))
    return pl.pallas_call(
        unpack_kernel,
        grid=(PARTS,),
        in_specs=[whole((n, part)), whole((rows, 1)), col],
        out_specs=[col, whole((rows, 1))],
        out_shape=[
            jax.ShapeDtypeStruct((rows, part * PARTS), BF16),
            jax.ShapeDtypeStruct((rows, 1), F32),
        ],
        compiler_params=params(),
        cost_estimate=pl.CostEstimate(
            flops=2 * n * rows * part * PARTS,
            bytes_accessed=6 * rows * part * PARTS,
            transcendentals=0,
        ),
        name="unpack",
    )(got, place_col, q)


def weigh_kernel(
    scale, got_ref, place_ref, prow_ref, q_ref, first_ref, stat_ref, packed_ref,
    f_ref, sent_ref, wcol_ref, norm_ref, vec_ref, hard, lossv,
):
    i = pl.program_id(0)
    rows = q_ref.shape[0]

    @pl.when(i == 0)
    def _():
        hard[...] = first_ref[...]

    @pl.when(i < PARTS)
    def _():
        lane = iota((rows, got_ref.shape[0]), 1)
        hit = jnp.where(lane == place_ref[...] + CAP * i, 1.0, 0.0).astype(BF16)
        fetched = dot(hit, got_ref[...])
        f_ref[...] = fetched.astype(BF16)
        hard[...] += jnp.sum(fetched * q_ref[...].astype(F32), axis=1, keepdims=True)

    @pl.when(i == PARTS - 1)
    def _():
        score = hard[...] * scale
        top_in, total_in, diag = stat_ref[:, 0:1], stat_ref[:, 1:2], stat_ref[:, 2:3]
        top = jnp.maximum(top_in, score)
        norm = top + jnp.log(total_in * jnp.exp(top_in - top) + jnp.exp(score - top))
        weight = jnp.exp(score - norm).astype(BF16).astype(F32)
        wcol_ref[...] = weight
        norm_ref[...] = norm
        eye = iota((rows, rows), 0) == iota((rows, rows), 1)
        vec_ref[0:1, :] = jnp.sum(jnp.where(eye, norm, 0.0), axis=0, keepdims=True)
        vec_ref[1:2, :] = jnp.sum(jnp.where(eye, weight, 0.0), axis=0, keepdims=True)
        vec_ref[2:8, :] = jnp.zeros((6, rows), F32)
        loss = jnp.sum(norm - diag, axis=0, keepdims=True)
        high = loss.astype(BF16).astype(F32)
        mid = (loss - high).astype(BF16).astype(F32)
        low = loss - high - mid
        at = iota((1, 128), 1)
        lossv[...] = jnp.where(
            at == 0, high, jnp.where(at == 1, mid, jnp.where(at == 2, low, 0.0))
        )

    @pl.when(i >= PARTS)
    def _():
        tile, part = packed_ref.shape
        row = (i - PARTS) * tile + iota((tile, rows), 0)
        slot = row - CAP * lax.rem(lax.div(row, CAP), PARTS)
        weight = jnp.sum(
            jnp.where(slot == prow_ref[...], vec_ref[1:2, :], 0.0), axis=1, keepdims=True
        )
        sent_ref[:, :part] = (packed_ref[...].astype(F32) * weight).astype(BF16)
        row = (i - PARTS) * tile + iota((tile, 128), 0)
        first = lax.rem(row, CAP * PARTS) == 0
        sent_ref[:, part:] = jnp.where(first, lossv[...], 0.0).astype(BF16)


def weigh(scale, got, place_col, place_row, q, first, stats, packed):
    rows, width = q.shape
    n, part = got.shape
    tiles = 4
    tile = n // tiles
    lanes = packed.shape[1]
    col = pl.BlockSpec((rows, part), lambda i: (0, PARTS + jnp.minimum(i, PARTS - 1)))
    out_col = pl.BlockSpec((rows, part), lambda i: (0, jnp.minimum(i, PARTS - 1)))

    def row_at(i):
        return (jnp.maximum(i - PARTS, 0), 0)

    return pl.pallas_call(
        functools.partial(weigh_kernel, scale),
        grid=(PARTS + tiles,),
        in_specs=[
            whole((n, part)),
            whole((rows, 1)),
            whole((1, rows)),
            col,
            whole((rows, 1)),
            whole((rows, 128)),
            pl.BlockSpec((tile, lanes), row_at),
        ],
        out_specs=[
            out_col,
            pl.BlockSpec((tile, lanes + 128), row_at),
            whole((rows, 1)),
            whole((rows, 1)),
            whole((8, rows)),
        ],
        out_shape=[
            jax.ShapeDtypeStruct((rows, part * PARTS), BF16),
            jax.ShapeDtypeStruct((n, lanes + 128), BF16),
            jax.ShapeDtypeStruct((rows, 1), F32),
            jax.ShapeDtypeStruct((rows, 1), F32),
            jax.ShapeDtypeStruct((8, rows), F32),
        ],
        scratch_shapes=[pltpu.VMEM((rows, 1), F32), pltpu.VMEM((1, 128), F32)],
        compiler_params=params(),
        cost_estimate=pl.CostEstimate(
            flops=2 * n * rows * part * PARTS,
            bytes_accessed=8 * rows * width,
            transcendentals=4 * rows,
        ),
        name="weigh",
    )(got, place_col, place_row, q, first, stats, packed)


def qgrad_kernel(s_ref, norm_ref, wcol_ref, p0, p1, p2, p3, f0, f1, out_ref, w):
    t = pl.program_id(0)
    rows = out_ref.shape[0]

    @pl.when(t == 0)
    def _():
        for j in range(4):
            v = jnp.exp(s_ref[:, j * rows : (j + 1) * rows] - norm_ref[...])
            if j == 0:
                eye = iota((rows, rows), 0) == iota((rows, rows), 1)
                v = jnp.where(eye, v - 1.0, v)
            w[:, j * rows : (j + 1) * rows] = v.astype(BF16)

    fetched = jnp.where(t < PARTS, f0[...].astype(F32), f1[...].astype(F32))
    acc = wcol_ref[...] * fetched
    for j, p in enumerate((p0, p1, p2, p3)):
        acc += dot(w[:, j * rows : (j + 1) * rows], p[...])
    out_ref[...] = acc


def qgrad(s, norm, wcol, passages, fetched):
    rows, width = passages[0].shape
    tile = width // (2 * PARTS)
    col = pl.BlockSpec((rows, tile), lambda t: (0, t))
    low = pl.BlockSpec((rows, tile), lambda t: (0, jnp.minimum(t, PARTS - 1)))
    high = pl.BlockSpec((rows, tile), lambda t: (0, jnp.maximum(t - PARTS, 0)))
    return pl.pallas_call(
        qgrad_kernel,
        grid=(2 * PARTS,),
        in_specs=[whole(s.shape), whole((rows, 1)), whole((rows, 1))] + [col] * 4 + [low, high],
        out_specs=col,
        out_shape=jax.ShapeDtypeStruct((rows, width), F32),
        scratch_shapes=[pltpu.VMEM((rows, 4 * rows), BF16)],
        compiler_params=params(),
        cost_estimate=pl.CostEstimate(
            flops=8 * rows * rows * width,
            bytes_accessed=14 * rows * width,
            transcendentals=4 * rows * rows,
        ),
        name="qgrad",
    )(s, norm, wcol, *passages, *fetched)


def pgrad_kernel(scale, p_ref, q0, q1, q2, q3, n0, n1, n2, n3, out_ref, wt):
    t = pl.program_id(0)
    rows = p_ref.shape[0]
    tile = out_ref.shape[1]
    queries = (q0, q1, q2, q3)

    @pl.when(t == 0)
    def _():
        for j, (q, norm) in enumerate(zip(queries, (n0, n1, n2, n3))):
            w = jnp.exp(dot_t(p_ref[...], q[...]) * scale - norm[0:1, :])
            if j == 0:
                eye = iota((rows, rows), 0) == iota((rows, rows), 1)
                w = jnp.where(eye, w - 1.0, w)
            wt[:, j * rows : (j + 1) * rows] = w.astype(BF16)

    at = pl.ds(pl.multiple_of(t * tile, tile), tile)
    acc = jnp.zeros(out_ref.shape, F32)
    for j, q in enumerate(queries):
        acc += dot(wt[:, j * rows : (j + 1) * rows], q[:, at])
    out_ref[...] = acc


def pgrad(scale, p, queries, norms):
    rows, width = p.shape
    tile = width // 8
    full = whole((rows, width))
    return pl.pallas_call(
        functools.partial(pgrad_kernel, scale),
        grid=(8,),
        in_specs=[full] * 5 + [whole((8, rows))] * 4,
        out_specs=pl.BlockSpec((rows, tile), lambda t: (0, t)),
        out_shape=jax.ShapeDtypeStruct((rows, width), F32),
        scratch_shapes=[pltpu.VMEM((rows, 4 * rows), BF16)],
        compiler_params=params(),
        cost_estimate=pl.CostEstimate(
            flops=16 * rows * rows * width,
            bytes_accessed=14 * rows * width,
            transcendentals=4 * rows * rows,
        ),
        name="pgrad",
    )(p, *queries, *norms)


def loss_kernel(got_ref, out_ref):
    both = jnp.sum(got_ref[...].astype(F32), axis=0, keepdims=True)
    out_ref[...] = jnp.broadcast_to(jnp.sum(both, axis=1, keepdims=True), out_ref.shape)


def losses(got, part):
    n = got.shape[0]
    return pl.pallas_call(
        loss_kernel,
        grid=(1,),
        in_specs=[pl.BlockSpec((n, 128), lambda i: (0, part // 128))],
        out_specs=whole((8, 128)),
        out_shape=jax.ShapeDtypeStruct((8, 128), F32),
        compiler_params=params(),
        name="losses",
    )(got)


def finish_kernel(code_ref, got_ref, part_ref, out_ref):
    k = pl.program_id(0)
    rows, part = out_ref.shape
    hit = jnp.where(
        code_ref[...] == iota((rows, code_ref.shape[1]), 0) + rows * k, 1.0, 0.0
    ).astype(BF16)
    out_ref[...] = part_ref[...] + dot(hit, got_ref[...])


def finish(codes_row, got, partial_grad):
    rows, width = partial_grad.shape
    part = width // PARTS
    col = pl.BlockSpec((rows, part), lambda k: (0, k))
    return pl.pallas_call(
        finish_kernel,
        grid=(PARTS,),
        in_specs=[whole(codes_row.shape), whole((got.shape[0], part)), col],
        out_specs=col,
        out_shape=jax.ShapeDtypeStruct((rows, width), F32),
        compiler_params=params(),
        cost_estimate=pl.CostEstimate(
            flops=2 * got.shape[0] * rows * width, bytes_accessed=9 * rows * width, transcendentals=0
        ),
        name="finish",
    )(codes_row, got, partial_grad)


def shards(queries, passages, hard_owner, hard_row):
    rows, width = queries.shape
    n_dp = lax.axis_size("dp")
    n_blk = lax.axis_size("blk")
    scale = 2.0 / math.sqrt(width)
    half = lax.rem(lax.axis_index("dp") // 4, 2).astype(jnp.int32)
    chunk = CAP * PARTS
    n = n_dp * chunk

    def permute(x, table):
        return lax.ppermute(x, "blk", table)

    def exchange(x, groups):
        return lax.all_to_all(x, ("dp", "blk"), 0, 0, axis_index_groups=groups, tiled=True)

    p_halves = [passages[:, : width // 2], passages[:, width // 2 :]]
    pair_halves = [permute(p, PAIR) for p in p_halves]
    p_core = permute(passages, CORE)

    owner = hard_owner[:, 0]
    row = hard_row[:, 0]
    hits = (owner[:, None] == jnp.arange(n_dp, dtype=jnp.int32)[None, :]).astype(BF16)
    order = jnp.arange(rows, dtype=jnp.int32)
    before = (order[:, None] > order[None, :]).astype(BF16)
    slot = jnp.sum(dot(before, hits) * hits.astype(F32), axis=1).astype(jnp.int32)
    place = owner * chunk + slot
    place_col, place_row = place.reshape(rows, 1), place.reshape(1, rows)
    at = jnp.arange(n, dtype=jnp.int32)
    part_of = (at // CAP) % PARTS
    match = (at - CAP * part_of)[:, None] == place[None, :]
    codes = jnp.sum(jnp.where(match, row[None, :] + 1, 0), axis=1)
    codes = jnp.where(codes > 0, codes - 1 + rows * part_of, -1)
    groups = neighbour_groups()
    asked = exchange(codes.reshape(n_dp, chunk), groups).reshape(n)
    asked_col = asked.reshape(n, 1)
    asked_pair = permute(asked, PAIR)

    here, there = half.reshape(1), (1 - half).reshape(1)
    own_part = [serve(here, asked_col, p) for p in p_halves]
    got = [
        exchange(serve(there, asked_col, p, o), groups) for p, o in zip(pair_halves, own_part)
    ]

    q_late, _ = lax.optimization_barrier((queries, asked_pair))
    q_pair = permute(q_late, PAIR)
    q_core = permute(queries, CORE)
    q_diag = permute(q_pair, CORE)

    p_pair = jnp.concatenate(pair_halves, axis=1)
    p_diag = permute(p_pair, CORE)
    passage_blocks = (passages, p_core, p_pair, p_diag)
    packed = pack(place_row, queries, n)
    s, stats = scores(scale, queries, passage_blocks)
    fetched0, first = unpack(got[0], place_col, queries)
    fetched1, sent, wcol, norm, vectors = weigh(
        scale, got[1], place_col, place_row, queries, first, stats, packed
    )
    terms = lax.all_to_all(sent, "dp", 0, 0, tiled=True)

    norms = (vectors, permute(vectors, CORE), permute(vectors, PAIR), permute(vectors, DIAG))
    query_gradient = qgrad(s, norm, wcol, passage_blocks, (fetched0, fetched1))
    partial_grad = pgrad(scale, passages, (queries, q_core, q_pair, q_diag), norms)

    loss_dp = losses(terms, width // PARTS)
    loss_all = loss_dp + permute(loss_dp, CORE) + permute(loss_dp, PAIR) + permute(loss_dp, DIAG)
    loss = loss_all[0, 0] / (rows * n_blk * n_dp)

    source_half = (at // chunk // 4) % 2
    owned = jnp.where(source_half == half, asked, asked_pair)
    passage_gradient = finish(owned.reshape(1, n), terms, partial_grad)
    return query_gradient, passage_gradient, loss


def solution(mesh):
    spec = P(("dp", "blk"), None)
    return jax.shard_map(
        shards,
        mesh=mesh,
        in_specs=(spec,) * 4,
        out_specs=(spec, spec, P()),
        check_vma=False,
    )
```

time: 381 us -> 187 us (0.49)
  blocking collectives: 166 us -> 0 us
  Pallas kernels: 0 us -> 77.6 us
  waiting for transfers between devices: 101 us -> 38.8 us
  matrix products: 29.6 us -> 0.2 us
  starting transfers between devices: 18.1 us -> 47.5 us
  local copies, waits for them, and re-layouts: 29.9 us -> 14 us
  other arithmetic: 18.6 us -> 3.97 us
  between operations: 16 us -> 2.74 us
    psum x1 -> x0, blocking collectives: 148 us -> none  [shards(): loss_total = lax.psum(jnp.sum(log_norm - positive), ('dp', 'blk'))]
    all_to_all x2 -> x4, waiting for transfers between devices: 87.1 us -> 6.88 us  [the longest x3 6.87 us: exchange(): lax.all_to_all(x, ('dp', 'blk'), 0, 0, axis_index_groups=groups, tiled=True)]
    pallas_call x0 -> x12, Pallas kernels: none -> 77.6 us  [the longest x4 17.1 us: serve(): pl.pallas_call(serve_kernel, grid_spec=pltpu.PrefetchScalarGridSpec(num_s...]
    ppermute x0 -> x14, waiting for transfers between devices: none -> 31.9 us  [permute(): return lax.ppermute(x, 'blk', table)]
    dot_general x4 -> x1, matrix products: 29.6 us -> 0.2 us  [dot(): return jnp.dot(a, b, preferred_element_type=F32)]
    all_to_all x2 -> x4, starting transfers between devices: 17.9 us -> 38.3 us  [the longest x3 28.3 us: exchange(): lax.all_to_all(x, ('dp', 'blk'), 0, 0, axis_index_groups=groups, tiled=True)]
    all_to_all x1 -> x0, blocking collectives: 17.9 us -> none  [shards(): lax.all_to_all(requests, 'dp', split_axis=0, concat_axis=0, tiled=True)]
    gather x4 -> x0, local copies, waits for them, and re-layouts: 16 us -> none  [the longest x2 8.45 us: shards(): picked = jnp.take(passages, asked_rows, axis=0)]
  transfers between devices with their start and end apart: 4 -> 18, of which waited for: 2 -> 4; matrix products, arithmetic and copies ran while one was open for 13% -> 6% of each run, Pallas kernels for 0% -> 41%
where the time goes in v1:
time: 187 us; the launch traced here: 185 us
  Pallas kernels  77.6 us (41%)
  starting transfers between devices  47.5 us (25%)
  waiting for transfers between devices  38.8 us (21%)
  local copies, waits for them, and re-layouts  14 us (7%)
  other arithmetic  3.97 us (2%)
  between operations  2.74 us (1%)
    ppermute x14, waiting for transfers between devices, permute(): return lax.ppermute(x, 'blk', table)  31.9 us
    all_to_all x3, starting transfers between devices, exchange(): lax.all_to_all(x, ('dp', 'blk'), 0, 0, axis_index_groups=groups, tiled=True)  28.3 us
    pallas_call x4, Pallas kernels, serve(): pl.pallas_call(serve_kernel, grid_spec=pltpu.PrefetchScalarGridSpec(num_s...  17.1 us
    pallas_call x1, Pallas kernels, pgrad(): pl.pallas_call(functools.partial(pgrad_kernel, scale), grid=(8,), in_spec...  12.2 us
    pallas_call x1, Pallas kernels, qgrad(): pl.pallas_call(qgrad_kernel, grid=(2 * PARTS,), in_specs=[whole(s.shape),...  10.1 us
    all_to_all x1, starting transfers between devices, shards(): terms = lax.all_to_all(sent, 'dp', 0, 0, tiled=True)  9.94 us
    pallas_call x1, Pallas kernels, weigh(): pl.pallas_call(functools.partial(weigh_kernel, scale), grid=(PARTS + tile...  9.37 us
    ppermute x14, starting transfers between devices, permute(): return lax.ppermute(x, 'blk', table)  9.22 us
  transfers between devices with their start and end apart: 18, of which 4 were waited for; matrix products, arithmetic and copies ran while one was open for 6% of the time, Pallas kernels for 41%

profile of v1, /device:TPU:4, one launch (start us, length us, event | category | flops | bytes accessed | tf_op | source)
XLA Modules:
  0.0 184.8 jit_solution(8452700516904771073)
XLA Ops:
  0.7 3.2 %fusion.20 = (bf16[256,2048]{1,0:T(8,128)(2,1)}, bf16[256,2048]{1,0:T(8,128)(2,1)}) fusion(bf16[256,4096]{1,0:T(8,128)(2,1)} %p_ref.1), kind=kLoop, calls=%fused_computation.59 | loop fusion | bytes 4194304 | tf_op jit(solution)/shard_map/slice | solution.py:445
  7.5 9.6 %all-to-all-start = ((s32[32,1,40]{2,1,0:T(1,128)}), s32[32,1,40]{2,1,0:T(1,128)S(1)}, u32[]{:S(2)}, u32[]{:S(2)}) async-start(s32[32,1,40]{2,1,0:T(1,128)} %bitcast.3), calls=%async_computation | async-start | bytes 32768 | tf_op jit(solution)/shard_map/all_to_all | solution.py:443
  17.2 6.9 %all-to-all-done = s32[32,1,40]{2,1,0:T(1,128)S(1)} async-done(((s32[32,1,40]{2,1,0:T(1,128)}), s32[32,1,40]{2,1,0:T(1,128)S(1)}, u32[]{:S(2)}, u32[]{:S(2)}) %all-to-all-start) | async-done | bytes 5152 | tf_op jit(solution)/shard_map/all_to_all | solution.py:443
  26.4 4.3 %serve.6.refs_0_ = bf16[1280,512]{1,0:T(8,128)(2,1)} custom-call(s32[1]{0:T(128)} %bitcast.4.half_ref, s32[1280,1]{1,0:T(8,128)} %reshape_reshape.4.code_ref, bf16[256,2048]{1,0:T(8,128)(2,1)} %get-tuple-element.24.src_ref), custom_call_target="tpu_custom_call" | custom-call | flops 671088640 | bytes 2097152 | tf_op jit(solution)/shard_map/serve/pallas_call | solution.py:71
  30.7 4.3 %serve.7 = bf16[1280,512]{1,0:T(8,128)(2,1)} custom-call(s32[1]{0:T(128)} %bitcast.half_ref, s32[1280,1]{1,0:T(8,128)} %reshape_reshape.4.code_ref, bf16[256,2048]{1,0:T(8,128)(2,1)} %collective-permute-done.1.src_ref, bf16[1280,512]{1,0:T(8,128)(2,1)} %serve.6.refs_0_), custom_call_target="tpu_custom_call", output_to_operand_aliasing={{}: (3, {})} | custom-call | flops 671088640 | bytes 2097152 | tf_op jit(solution)/shard_map/serve/pallas_call | solution.py:71
  35.0 9.2 %all-to-all-start.2 = ((bf16[32,40,512]{2,1,0:T(8,128)(2,1)}), bf16[32,40,512]{2,1,0:T(8,128)(2,1)}, u32[]{:S(2)}, u32[]{:S(2)}) async-start(bf16[32,40,512]{2,1,0:T(8,128)(2,1)} %bitcast.18), calls=%async_computation.2 | async-start | bytes 2621440 | tf_op jit(solution)/shard_map/all_to_all | solution.py:443
  44.2 2.4 %constant_dynamic-update-slice_fusion.1 = bf16[256,4096]{1,0:T(8,128)(2,1)} fusion(bf16[256,2048]{1,0:T(8,128)(2,1)} %collective-permute-done.1.src_ref), kind=kLoop, calls=%fused_computation.53 | loop fusion | bytes 2097152
  46.5 5.0 %collective-permute-done.2.src_ref = bf16[256,2048]{1,0:T(8,128)(2,1)S(1)} collective-permute-done((bf16[256,2048]{1,0:T(8,128)(2,1)}, bf16[256,2048]{1,0:T(8,128)(2,1)S(1)}, u32[]{:S(2)}, u32[]{:S(2)}) %collective-permute-start.2) | collective-permute-done | bytes 1048608 | tf_op jit(solution)/shard_map/ppermute | solution.py:440
  54.0 2.5 %collective-permute-done.4 = s32[1280]{0:T(1024)S(1)} collective-permute-done((s32[1280]{0:T(1024)S(1)}, s32[1280]{0:T(1024)S(1)}, u32[]{:S(2)}, u32[]{:S(2)}) %collective-permute-start.4) | collective-permute-done | bytes 5152 | tf_op jit(solution)/shard_map/ppermute | solution.py:440
  57.6 4.3 %serve.4.refs_0_ = bf16[1280,512]{1,0:T(8,128)(2,1)} custom-call(s32[1]{0:T(128)} %bitcast.4.half_ref, s32[1280,1]{1,0:T(8,128)} %reshape_reshape.4.code_ref, bf16[256,2048]{1,0:T(8,128)(2,1)} %get-tuple-element.23.src_ref), custom_call_target="tpu_custom_call" | custom-call | flops 671088640 | bytes 2097152 | tf_op jit(solution)/shard_map/serve/pallas_call | solution.py:71
  61.9 4.3 %serve.5 = bf16[1280,512]{1,0:T(8,128)(2,1)} custom-call(s32[1]{0:T(128)} %bitcast.half_ref, s32[1280,1]{1,0:T(8,128)} %reshape_reshape.4.code_ref, bf16[256,2048]{1,0:T(8,128)(2,1)} %copy-done.3, bf16[1280,512]{1,0:T(8,128)(2,1)} %serve.4.refs_0_), custom_call_target="tpu_custom_call", output_to_operand_aliasing={{}: (3, {})} | custom-call | flops 671088640 | bytes 2097152 | tf_op jit(solution)/shard_map/serve/pallas_call | solution.py:71
  66.2 9.6 %all-to-all-start.1 = ((bf16[32,40,512]{2,1,0:T(8,128)(2,1)}), bf16[32,40,512]{2,1,0:T(8,128)(2,1)S(1)}, u32[]{:S(2)}, u32[]{:S(2)}) async-start(bf16[32,40,512]{2,1,0:T(8,128)(2,1)} %bitcast.19), calls=%async_computation.1 | async-start | bytes 2621440 | tf_op jit(solution)/shard_map/all_to_all | solution.py:443
  78.8 7.1 %pack.1.packed_ref = bf16[1280,1024]{1,0:T(8,128)(2,1)} custom-call(s32[1,256]{1,0:T(1,128)} %add.120.place_ref.prow_ref, bf16[256,4096]{1,0:T(8,128)(2,1)} %q0.1), custom_call_target="tpu_custom_call" | custom-call | flops 2684354560 | bytes 4194304 | tf_op jit(solution)/shard_map/pack/pallas_call | solution.py:105
  85.9 5.2 %unpack.1 = (bf16[256,2048]{1,0:T(8,128)(2,1)}, f32[256,1]{1,0:T(8,128)}) custom-call(bf16[1280,512]{1,0:T(8,128)(2,1)} %bitcast.10.got_ref, s32[256,1]{1,0:T(8,128)} %get-tuple-element.26.place_ref, bf16[256,4096]{1,0:T(8,128)(2,1)} %q0.1), custom_call_target="tpu_custom_call" | custom-call | flops 1342177280 | bytes 3145728 | tf_op jit(solution)/shard_map/unpack/pallas_call | solution.py:176
  91.2 7.5 %scores.1 = (f32[256,1024]{1,0:T(8,128)}, f32[256,128]{1,0:T(8,128)}) custom-call(bf16[256,4096]{1,0:T(8,128)(2,1)} %q0.1, bf16[256,4096]{1,0:T(8,128)(2,1)} %p_ref.1, bf16[256,4096]{1,0:T(8,128)(2,1)} %collective-permute-done.p1, bf16[256,4096]{1,0:T(8,128)(2,1)} %constant_dynamic-update-slice_fusion.p2, bf16[256,4096]{1,0:T(8,128)(2,1)} %collective-permute-done.3.p3), custom_call_target="tpu_custom_call" | custom-call | flops 2147483648 | bytes 10485760 | tf_op jit(solution)/shard_map/scores/pallas_call | solution.py:138
  99.7 9.4 %weigh.1 = (bf16[256,2048]{1,0:T(8,128)(2,1)}, bf16[1280,1152]{1,0:T(8,128)(2,1)}, f32[256,1]{1,0:T(8,128)}, f32[256,1]{1,0:T(8,128)}, f32[8,256]{1,0:T(8,128)}) custom-call(bf16[1280,512]{1,0:T(8,128)(2,1)} %bitcast.20, s32[256,1]{1,0:T(8,128)} %get-tuple-element.26.place_ref, s32[1,256]{1,0:T(1,128)} %add.120.place_ref.prow_ref, bf16[256,4096]{1,0:T(8,128)(2,1)} %q0.1, ...), custom_call_target="tpu_custom_call" | custom-call | flops 1342177280 | bytes 8388608 | tf_op jit(solution)/shard_map/weigh/pallas_call | solution.py:262
  109.1 9.9 %all-to-all-start.3 = ((bf16[32,40,1152]{2,1,0:T(8,128)(2,1)}), bf16[32,40,1152]{2,1,0:T(8,128)(2,1)S(1)}, u32[]{:S(2)}, u32[]{:S(2)}) async-start(bf16[32,40,1152]{2,1,0:T(8,128)(2,1)} %bitcast.21), calls=%async_computation.3 | async-start | bytes 5898240 | tf_op jit(solution)/shard_map/all_to_all | solution.py:487
  120.4 2.0 %collective-permute-start.9 = (f32[8,256]{1,0:T(8,128)S(1)}, f32[8,256]{1,0:T(8,128)S(1)}, u32[]{:S(2)}, u32[]{:S(2)}) collective-permute-start(f32[8,256]{1,0:T(8,128)S(1)} %copy-done.10), channel_id=1, source_target_pairs={{0,2},{1,3},{2,0},{3,1},{4,6},{5,7},{6,4},{7,5},{8,10},{9,11},{10,... | collective-permute-start | bytes 24584 | tf_op jit(solution)/shard_map/ppermute | solution.py:440
  122.4 10.1 %qgrad.1 = f32[256,4096]{1,0:T(8,128)} custom-call(f32[256,1024]{1,0:T(8,128)} %get-tuple-element.13.s_ref, f32[256,1]{1,0:T(8,128)} %get-tuple-element.16.norm_ref, f32[256,1]{1,0:T(8,128)} %get-tuple-element.17.wcol_ref, bf16[256,4096]{1,0:T(8,128)(2,1)} %p_ref.1, bf16[256,4096]{1,0:T(8,128)(2,1)} %collective-permute-done.p1, ...), custom_call_target="tpu_custom_call" | custom-call | flops 2147483648 | bytes 14680064 | tf_op jit(solution)/shard_map/qgrad/pallas_call | solution.py:325
  132.6 24.4 %collective-permute-done.9.n2 = f32[8,256]{1,0:T(8,128)S(1)} collective-permute-done((f32[8,256]{1,0:T(8,128)S(1)}, f32[8,256]{1,0:T(8,128)S(1)}, u32[]{:S(2)}, u32[]{:S(2)}) %collective-permute-start.9) | collective-permute-done | bytes 8224 | tf_op jit(solution)/shard_map/ppermute | solution.py:440
  157.6 12.2 %pgrad.1.part_ref = f32[256,4096]{1,0:T(8,128)} custom-call(bf16[256,4096]{1,0:T(8,128)(2,1)} %p_ref.1, bf16[256,4096]{1,0:T(8,128)(2,1)} %q0.1, bf16[256,4096]{1,0:T(8,128)(2,1)} %copy-done.9, bf16[256,4096]{1,0:T(8,128)(2,1)} %collective-permute-done.6.q2, bf16[256,4096]{1,0:T(8,128)(2,1)} %collective-permute-done.7.q3, f32[8,256]{1,0:T(8,128)} %get-tuple-element.22.n0, ...), custom_call_target="tpu_custom_call" | custom-call | flops 4294967296 | bytes 14680064 | tf_op jit(solution)/shard_map/pgrad/pallas_call | solution.py:368
  171.4 1.8 losses.1
  173.3 1.7 collective-permute-start.12
  175.1 7.3 %finish.1 = f32[256,4096]{1,0:T(8,128)} custom-call(s32[1,1280]{1,0:T(1,128)} %reshape.212.code_ref, bf16[1280,1152]{1,0:T(8,128)(2,1)} %bitcast.17, f32[256,4096]{1,0:T(8,128)} %pgrad.1.part_ref), custom_call_target="tpu_custom_call" | custom-call | flops 2684354560 | bytes 9437184 | tf_op jit(solution)/shard_map/finish/pallas_call | solution.py:416
  (78 shorter events, 18.1 us)
Async XLA Ops:
  0.6 16.4 %copy-start.1 = (bf16[256,4096]{1,0:T(8,128)(2,1)S(1)}, bf16[256,4096]{1,0:T(8,128)(2,1)}, u32[]{:S(2)}) copy-start(bf16[256,4096]{1,0:T(8,128)(2,1)} %p_ref.1) | copy-start | bytes 6291460
  3.9 26.8 %collective-permute-start.1 = (bf16[256,2048]{1,0:T(8,128)(2,1)}, bf16[256,2048]{1,0:T(8,128)(2,1)}, u32[]{:S(2)}, u32[]{:S(2)}) collective-permute-start(bf16[256,2048]{1,0:T(8,128)(2,1)} %get-tuple-element.24.src_ref), channel_id=1, source_target_pairs={{0,2},{1,3},{2,0},{3,1},{4,6},{5,7},{6,4},{7,5},{8,10},{9,11},{10,... | collective-permute-start | bytes 3145736 | tf_op jit(solution)/shard_map/ppermute | solution.py:440
  5.1 46.4 %collective-permute-start.2 = (bf16[256,2048]{1,0:T(8,128)(2,1)}, bf16[256,2048]{1,0:T(8,128)(2,1)S(1)}, u32[]{:S(2)}, u32[]{:S(2)}) collective-permute-start(bf16[256,2048]{1,0:T(8,128)(2,1)} %get-tuple-element.23.src_ref), channel_id=1, source_target_pairs={{0,2},{1,3},{2,0},{3,1},{4,6},{5,7},{6,4},{7,5},{8,10},{9,11},{10,... | collective-permute-start | bytes 3145736 | tf_op jit(solution)/shard_map/ppermute | solution.py:440
  7.5 16.6 %all-to-all-start = ((s32[32,1,40]{2,1,0:T(1,128)}), s32[32,1,40]{2,1,0:T(1,128)S(1)}, u32[]{:S(2)}, u32[]{:S(2)}) async-start(s32[32,1,40]{2,1,0:T(1,128)} %bitcast.3), calls=%async_computation | async-start | bytes 32768 | tf_op jit(solution)/shard_map/all_to_all | solution.py:443
  17.1 74.1 %collective-permute-start = (bf16[256,4096]{1,0:T(8,128)(2,1)S(1)}, bf16[256,4096]{1,0:T(8,128)(2,1)}, u32[]{:S(2)}, u32[]{:S(2)}) collective-permute-start(bf16[256,4096]{1,0:T(8,128)(2,1)S(1)} %copy-done.1), channel_id=1, source_target_pairs={{0,1},{1,0},{2,3},{3,2},{4,5},{5,4},{6,7},{7,6},{8,9},{9,8},{10,11... | collective-permute-start | bytes 6291464 | tf_op jit(solution)/shard_map/ppermute | solution.py:440
  35.0 31.2 %all-to-all-start.2 = ((bf16[32,40,512]{2,1,0:T(8,128)(2,1)}), bf16[32,40,512]{2,1,0:T(8,128)(2,1)}, u32[]{:S(2)}, u32[]{:S(2)}) async-start(bf16[32,40,512]{2,1,0:T(8,128)(2,1)} %bitcast.18), calls=%async_computation.2 | async-start | bytes 2621440 | tf_op jit(solution)/shard_map/all_to_all | solution.py:443
  51.5 10.4 %copy-start.3 = (bf16[256,2048]{1,0:T(8,128)(2,1)}, bf16[256,2048]{1,0:T(8,128)(2,1)S(1)}, u32[]{:S(2)}) copy-start(bf16[256,2048]{1,0:T(8,128)(2,1)S(1)} %collective-permute-done.2.src_ref) | copy-start | bytes 3145732
  52.6 38.6 %collective-permute-start.3 = (bf16[256,4096]{1,0:T(8,128)(2,1)}, bf16[256,4096]{1,0:T(8,128)(2,1)}, u32[]{:S(2)}, u32[]{:S(2)}) collective-permute-start(bf16[256,4096]{1,0:T(8,128)(2,1)} %constant_dynamic-update-slice_fusion.p2), channel_id=1, source_target_pairs={{0,1},{1,0},{2,3},{3,2},{4,5},{5,4},{6,7},{7,6},{8,9},{9,8},{10,11... | collective-permute-start | bytes 6291464 | tf_op jit(solution)/shard_map/ppermute | solution.py:440
  52.7 3.7 %collective-permute-start.4 = (s32[1280]{0:T(1024)S(1)}, s32[1280]{0:T(1024)S(1)}, u32[]{:S(2)}, u32[]{:S(2)}) collective-permute-start(s32[1280]{0:T(1024)S(1)} %reshape.211), channel_id=1, source_target_pairs={{0,2},{1,3},{2,0},{3,1},{4,6},{5,7},{6,4},{7,5},{8,10},{9,11},{10,... | collective-permute-start | bytes 15368 | tf_op jit(solution)/shard_map/ppermute | solution.py:440
  56.4 62.7 %collective-permute-start.6 = (bf16[256,4096]{1,0:T(8,128)(2,1)}, bf16[256,4096]{1,0:T(8,128)(2,1)}, u32[]{:S(2)}, u32[]{:S(2)}) collective-permute-start(bf16[256,4096]{1,0:T(8,128)(2,1)} %q0.1), channel_id=1, source_target_pairs={{0,2},{1,3},{2,0},{3,1},{4,6},{5,7},{6,4},{7,5},{8,10},{9,11},{10,... | collective-permute-start | bytes 6291464 | tf_op jit(solution)/shard_map/ppermute | solution.py:440
  66.2 32.5 %all-to-all-start.1 = ((bf16[32,40,512]{2,1,0:T(8,128)(2,1)}), bf16[32,40,512]{2,1,0:T(8,128)(2,1)S(1)}, u32[]{:S(2)}, u32[]{:S(2)}) async-start(bf16[32,40,512]{2,1,0:T(8,128)(2,1)} %bitcast.19), calls=%async_computation.1 | async-start | bytes 2621440 | tf_op jit(solution)/shard_map/all_to_all | solution.py:443
  109.1 10.6 %copy-start.6 = (s32[1280]{0:T(1024)S(1)}, s32[1280]{0:T(1024)}, u32[]{:S(2)}) copy-start(s32[1280]{0:T(1024)} %copy-done.5) | copy-start | bytes 15364
  109.1 11.2 %copy-start.10 = (f32[8,256]{1,0:T(8,128)S(1)}, f32[8,256]{1,0:T(8,128)}, u32[]{:S(2)}) copy-start(f32[8,256]{1,0:T(8,128)} %get-tuple-element.22.n0) | copy-start | bytes 24580
  109.1 60.7 %all-to-all-start.3 = ((bf16[32,40,1152]{2,1,0:T(8,128)(2,1)}), bf16[32,40,1152]{2,1,0:T(8,128)(2,1)S(1)}, u32[]{:S(2)}, u32[]{:S(2)}) async-start(bf16[32,40,1152]{2,1,0:T(8,128)(2,1)} %bitcast.21), calls=%async_computation.3 | async-start | bytes 5898240 | tf_op jit(solution)/shard_map/all_to_all | solution.py:487
  119.0 13.5 %collective-permute-start.5 = (bf16[256,4096]{1,0:T(8,128)(2,1)}, bf16[256,4096]{1,0:T(8,128)(2,1)S(1)}, u32[]{:S(2)}, u32[]{:S(2)}) collective-permute-start(bf16[256,4096]{1,0:T(8,128)(2,1)} %q0.1), channel_id=1, source_target_pairs={{0,1},{1,0},{2,3},{3,2},{4,5},{5,4},{6,7},{7,6},{8,9},{9,8},{10,11... | collective-permute-start | bytes 6291464 | tf_op jit(solution)/shard_map/ppermute | solution.py:440
  119.1 37.9 %collective-permute-start.7 = (bf16[256,4096]{1,0:T(8,128)(2,1)}, bf16[256,4096]{1,0:T(8,128)(2,1)}, u32[]{:S(2)}, u32[]{:S(2)}) collective-permute-start(bf16[256,4096]{1,0:T(8,128)(2,1)} %collective-permute-done.6.q2), channel_id=1, source_target_pairs={{0,1},{1,0},{2,3},{3,2},{4,5},{5,4},{6,7},{7,6},{8,9},{9,8},{10,11... | collective-permute-start | bytes 6291464 | tf_op jit(solution)/shard_map/ppermute | solution.py:440
  120.3 12.3 %collective-permute-start.8 = (f32[8,256]{1,0:T(8,128)S(1)}, f32[8,256]{1,0:T(8,128)S(1)}, u32[]{:S(2)}, u32[]{:S(2)}) collective-permute-start(f32[8,256]{1,0:T(8,128)S(1)} %copy-done.10), channel_id=1, source_target_pairs={{0,1},{1,0},{2,3},{3,2},{4,5},{5,4},{6,7},{7,6},{8,9},{9,8},{10,11... | collective-permute-start | bytes 24584 | tf_op jit(solution)/shard_map/ppermute | solution.py:440
  120.4 36.6 %collective-permute-start.9 = (f32[8,256]{1,0:T(8,128)S(1)}, f32[8,256]{1,0:T(8,128)S(1)}, u32[]{:S(2)}, u32[]{:S(2)}) collective-permute-start(f32[8,256]{1,0:T(8,128)S(1)} %copy-done.10), channel_id=1, source_target_pairs={{0,2},{1,3},{2,0},{3,1},{4,6},{5,7},{6,4},{7,5},{8,10},{9,11},{10,... | collective-permute-start | bytes 24584 | tf_op jit(solution)/shard_map/ppermute | solution.py:440
  122.4 34.6 %collective-permute-start.10 = (f32[8,256]{1,0:T(8,128)S(1)}, f32[8,256]{1,0:T(8,128)S(1)}, u32[]{:S(2)}, u32[]{:S(2)}) collective-permute-start(f32[8,256]{1,0:T(8,128)S(1)} %copy-done.10), channel_id=1, source_target_pairs={{0,3},{1,2},{2,1},{3,0},{4,7},{5,6},{6,5},{7,4},{8,11},{9,10},{10,... | collective-permute-start | bytes 24584 | tf_op jit(solution)/shard_map/ppermute | solution.py:440
  132.5 24.5 %copy-start.9 = (bf16[256,4096]{1,0:T(8,128)(2,1)}, bf16[256,4096]{1,0:T(8,128)(2,1)S(1)}, u32[]{:S(2)}) copy-start(bf16[256,4096]{1,0:T(8,128)(2,1)S(1)} %collective-permute-done.5.q1) | copy-start | bytes 6291460
  132.6 24.5 %copy-start.11 = (f32[8,256]{1,0:T(8,128)}, f32[8,256]{1,0:T(8,128)S(1)}, u32[]{:S(2)}) copy-start(f32[8,256]{1,0:T(8,128)S(1)} %collective-permute-done.8.n1) | copy-start | bytes 24580
  173.2 9.2 %collective-permute-start.13 = (f32[8,128]{1,0:T(8,128)}, f32[8,128]{1,0:T(8,128)S(1)}, u32[]{:S(2)}, u32[]{:S(2)}) collective-permute-start(f32[8,128]{1,0:T(8,128)} %losses.1), channel_id=1, source_target_pairs={{0,3},{1,2},{2,1},{3,0},{4,7},{5,6},{6,5},{7,4},{8,11},{9,10},{10,... | collective-permute-start | bytes 12296 | tf_op jit(solution)/shard_map/ppermute | solution.py:440
  173.3 9.2 %collective-permute-start.12 = (f32[8,128]{1,0:T(8,128)}, f32[8,128]{1,0:T(8,128)S(1)}, u32[]{:S(2)}, u32[]{:S(2)}) collective-permute-start(f32[8,128]{1,0:T(8,128)} %losses.1), channel_id=1, source_target_pairs={{0,2},{1,3},{2,0},{3,1},{4,6},{5,7},{6,4},{7,5},{8,10},{9,11},{10,... | collective-permute-start | bytes 12296 | tf_op jit(solution)/shard_map/ppermute | solution.py:440
  175.0 7.5 %collective-permute-start.11 = (f32[8,128]{1,0:T(8,128)}, f32[8,128]{1,0:T(8,128)S(1)}, u32[]{:S(2)}, u32[]{:S(2)}) collective-permute-start(f32[8,128]{1,0:T(8,128)} %losses.1), channel_id=1, source_target_pairs={{0,1},{1,0},{2,3},{3,2},{4,5},{5,4},{6,7},{7,6},{8,9},{9,8},{10,11... | collective-permute-start | bytes 12296 | tf_op jit(solution)/shard_map/ppermute | solution.py:440
  (8 other events, 33.7 us)

commit v2 on v1

v2 whole, which is shorter than its diff:
```python
import functools
import math

import jax
import jax.numpy as jnp
from jax import lax
from jax.experimental import pallas as pl
from jax.experimental.pallas import tpu as pltpu
from jax.sharding import PartitionSpec as P

MAIN, EXTRA = 8, 2
PARTS = 4
F32, BF16 = jnp.float32, jnp.bfloat16
VMEM_BYTES = 58 * 1024 * 1024
SMALL_BYTES = 32 * 1024 * 1024
PAIR = [(i, i ^ 2) for i in range(4)]
CORE = [(i, i ^ 1) for i in range(4)]
DIAG = [(i, i ^ 3) for i in range(4)]


def position(dp):
    return dp // 4 % 2 * 16 + dp // 8 * 4 + dp % 4


def order(core):
    return sorted(range(32), key=position, reverse=bool(core))


NEIGHBOURS = [
    [m * 4 + (a ^ (m // 4 % 2)) * 2 + core for m in order(core)] for a in range(2) for core in range(2)
]
COLUMNS = [[m * 4 + a * 2 + core for m in order(core)] for a in range(2) for core in range(2)]


def dot(a, b):
    return jnp.dot(a, b, preferred_element_type=F32)


def dot_t(a, b):
    return lax.dot_general(a, b, (((1,), (1,)), ((), ())), preferred_element_type=F32)


def iota(shape, dim):
    return lax.broadcasted_iota(jnp.int32, shape, dim)


def params(limit=VMEM_BYTES):
    return pltpu.CompilerParams(vmem_limit_bytes=limit)


def whole(shape):
    return pl.BlockSpec(shape, lambda *_: (0,) * len(shape))


def one(hit):
    return jnp.where(hit, 1.0, 0.0).astype(BF16)


def chunk_row(shape, dim):
    r = iota(shape, dim)
    return r, r - EXTRA * lax.div(lax.rem(r, MAIN), EXTRA)


def serve_kernel(half_ref, code_ref, own_ref, pair_ref, out_ref):
    rows, width = own_ref.shape
    part = width // PARTS
    half_rows = code_ref.shape[0] // 2
    lane = iota((half_rows, rows), 1)
    half = half_ref[0]
    for src, which in ((own_ref, half), (pair_ref, 1 - half)):
        at = pl.ds(pl.multiple_of(which * half_rows, half_rows), half_rows)
        code = code_ref[at, :]
        main = one(code[:, 0:1] == lane)
        acc = jnp.zeros((half_rows, part), F32)
        for k in range(PARTS):
            values = src[:, k * part : (k + 1) * part]
            out_ref[at, k * part : (k + 1) * part] = dot(main, values).astype(BF16)
            acc += dot(one(code[:, 1:2] == lane + rows * k), values)
        out_ref[at, width:] = acc.astype(BF16)


def serve(half, codes, own, pair):
    rows, width = own.shape
    n = codes.shape[0]
    lanes = width + width // PARTS
    return pl.pallas_call(
        serve_kernel,
        grid=(1,),
        in_specs=[pl.BlockSpec(memory_space=pltpu.SMEM)]
        + [whole(codes.shape), whole(own.shape), whole(pair.shape)],
        out_specs=whole((n, lanes)),
        out_shape=jax.ShapeDtypeStruct((n, lanes), BF16),
        compiler_params=params(),
        cost_estimate=pl.CostEstimate(
            flops=4 * n * rows * width, bytes_accessed=7 * rows * width, transcendentals=0
        ),
        name="serve",
    )(half, codes, own, pair)


def pack_kernel(place_ref, q_ref, out_ref, acc):
    k = pl.program_id(0)
    rows = q_ref.shape[0]
    n = out_ref.shape[0]

    @pl.when(k == 0)
    def _():
        acc[...] = jnp.zeros_like(acc)

    @pl.when(k < PARTS)
    def _():
        row = iota((n, rows), 0)
        out_ref[...] = dot(one(row == place_ref[0:1, :]), q_ref[...]).astype(BF16)
        acc[...] += dot(one(row == place_ref[1:2, :] + EXTRA * k), q_ref[...])

    @pl.when(k == PARTS)
    def _():
        out_ref[...] = acc[...].astype(BF16)


def pack(place_rows, q, n):
    rows, width = q.shape
    part = width // PARTS
    return pl.pallas_call(
        pack_kernel,
        grid=(PARTS + 1,),
        in_specs=[
            whole((2, rows)),
            pl.BlockSpec((rows, part), lambda k: (0, jnp.minimum(k, PARTS - 1))),
        ],
        out_specs=pl.BlockSpec((n, part), lambda k: (0, k)),
        out_shape=jax.ShapeDtypeStruct((n, width + part + 128), BF16),
        scratch_shapes=[pltpu.VMEM((n, part), F32)],
        compiler_params=params(),
        cost_estimate=pl.CostEstimate(
            flops=4 * n * rows * width, bytes_accessed=5 * rows * width, transcendentals=0
        ),
        name="pack",
    )(place_rows, q)


def scores_kernel(scale, q_ref, p0, p1, p2, p3, s_ref, stat_ref):
    rows = q_ref.shape[0]
    blocks = [dot_t(q_ref[...], p[...]) * scale for p in (p0, p1, p2, p3)]
    top = jnp.max(blocks[0], axis=1, keepdims=True)
    for b in blocks[1:]:
        top = jnp.maximum(top, jnp.max(b, axis=1, keepdims=True))
    total = jnp.zeros_like(top)
    for j, b in enumerate(blocks):
        total += jnp.sum(jnp.exp(b - top), axis=1, keepdims=True)
        s_ref[:, j * rows : (j + 1) * rows] = b
    eye = iota((rows, rows), 0) == iota((rows, rows), 1)
    diag = jnp.sum(jnp.where(eye, blocks[0], 0.0), axis=1, keepdims=True)
    lane = iota(stat_ref.shape, 1)
    stat_ref[...] = jnp.where(lane == 0, top, jnp.where(lane == 1, total, diag))


def scores(scale, q, passages):
    rows, width = q.shape
    full = whole((rows, width))
    return pl.pallas_call(
        functools.partial(scores_kernel, scale),
        grid=(1,),
        in_specs=[full] * 5,
        out_specs=[whole((rows, 4 * rows)), whole((rows, 128))],
        out_shape=[
            jax.ShapeDtypeStruct((rows, 4 * rows), F32),
            jax.ShapeDtypeStruct((rows, 128), F32),
        ],
        compiler_params=params(),
        cost_estimate=pl.CostEstimate(
            flops=8 * rows * rows * width,
            bytes_accessed=10 * rows * width,
            transcendentals=4 * rows * rows,
        ),
        name="scores",
    )(q, *passages)


def take_rows(got_ref, place_ref, q_ref, f_ref):
    rows, width = q_ref.shape
    part = width // PARTS
    lane = iota((rows, got_ref.shape[0]), 1)
    main = one(lane == place_ref[:, 0:1])
    score = jnp.zeros((rows, 1), F32)
    for k in range(PARTS):
        at = slice(k * part, (k + 1) * part)
        fetched = dot(main, got_ref[:, at])
        fetched += dot(one(lane == place_ref[:, 1:2] + EXTRA * k), got_ref[:, width:])
        f_ref[:, at] = fetched.astype(BF16)
        score += jnp.sum(fetched * q_ref[:, at].astype(F32), axis=1, keepdims=True)
    return score


def unpack_kernel(got_ref, place_ref, q_ref, f_ref, hard_ref):
    hard_ref[...] = take_rows(got_ref, place_ref, q_ref, f_ref)


def unpack(got, place_cols, q):
    rows, width = q.shape[0], q.shape[1] // 2
    return pl.pallas_call(
        unpack_kernel,
        grid=(1,),
        in_specs=[whole(got.shape), whole((rows, 2)), pl.BlockSpec((rows, width), lambda i: (0, 0))],
        out_specs=[whole((rows, width)), whole((rows, 1))],
        out_shape=[
            jax.ShapeDtypeStruct((rows, width), BF16),
            jax.ShapeDtypeStruct((rows, 1), F32),
        ],
        compiler_params=params(),
        cost_estimate=pl.CostEstimate(
            flops=4 * got.shape[0] * rows * width,
            bytes_accessed=7 * rows * width,
            transcendentals=0,
        ),
        name="unpack",
    )(got, place_cols, q)


def soft_kernel(
    scale, got_ref, place_ref, q_ref, first_ref, stat_ref, f_ref, wcol_ref, norm_ref, vec_ref
):
    rows = q_ref.shape[0]
    score = (first_ref[...] + take_rows(got_ref, place_ref, q_ref, f_ref)) * scale
    top_in, total_in, diag = stat_ref[:, 0:1], stat_ref[:, 1:2], stat_ref[:, 2:3]
    top = jnp.maximum(top_in, score)
    norm = top + jnp.log(total_in * jnp.exp(top_in - top) + jnp.exp(score - top))
    weight = jnp.exp(score - norm).astype(BF16).astype(F32)
    wcol_ref[...] = weight
    norm_ref[...] = norm
    eye = iota((rows, rows), 0) == iota((rows, rows), 1)
    vec_ref[0:1, :] = jnp.sum(jnp.where(eye, norm, 0.0), axis=0, keepdims=True)
    vec_ref[1:2, :] = jnp.sum(jnp.where(eye, weight, 0.0), axis=0, keepdims=True)
    loss = jnp.sum(norm - diag, axis=0, keepdims=True)
    vec_ref[2:3, :] = jnp.broadcast_to(loss, (1, rows))
    vec_ref[3:8, :] = jnp.zeros((5, rows), F32)


def soft(scale, got, place_cols, q, first, stats):
    rows, width = q.shape[0], q.shape[1] // 2
    return pl.pallas_call(
        functools.partial(soft_kernel, scale),
        grid=(1,),
        in_specs=[
            whole(got.shape),
            whole((rows, 2)),
            pl.BlockSpec((rows, width), lambda i: (0, 1)),
            whole((rows, 1)),
            whole((rows, 128)),
        ],
        out_specs=[whole((rows, width)), whole((rows, 1)), whole((rows, 1)), whole((8, rows))],
        out_shape=[
            jax.ShapeDtypeStruct((rows, width), BF16),
            jax.ShapeDtypeStruct((rows, 1), F32),
            jax.ShapeDtypeStruct((rows, 1), F32),
            jax.ShapeDtypeStruct((8, rows), F32),
        ],
        compiler_params=params(),
        cost_estimate=pl.CostEstimate(
            flops=4 * got.shape[0] * rows * width,
            bytes_accessed=7 * rows * width,
            transcendentals=4 * rows,
        ),
        name="soft",
    )(got, place_cols, q, first, stats)


def stamp_kernel(place_ref, v0, v1, v2, v3, packed_ref, out_ref):
    n, rows = out_ref.shape[0], place_ref.shape[1]
    row, base = chunk_row((n, rows), 0)
    weight = v0[1:2, :]
    main = jnp.sum(jnp.where(row == place_ref[0:1, :], weight, 0.0), axis=1, keepdims=True)
    extra = jnp.sum(jnp.where(base == place_ref[1:2, :], weight, 0.0), axis=1, keepdims=True)
    loss = v0[2:3, 0:128] + v1[2:3, 0:128] + v2[2:3, 0:128] + v3[2:3, 0:128]
    high = loss.astype(BF16).astype(F32)
    mid = (loss - high).astype(BF16).astype(F32)
    low = loss - high - mid
    lane = iota((1, 128), 1)
    parts = jnp.where(lane == 2, high, jnp.where(lane == 3, mid, jnp.where(lane == 4, low, 0.0)))
    first = lax.rem(iota(out_ref.shape, 0), MAIN) == 0
    lane = iota(out_ref.shape, 1)
    notes = jnp.where(lane == 0, main, jnp.where(lane == 1, extra, jnp.where(first, parts, 0.0)))
    out_ref[...] = notes.astype(BF16)


def stamp(place_rows, vectors, packed):
    n, lanes = packed.shape
    return pl.pallas_call(
        stamp_kernel,
        grid=(1,),
        in_specs=[whole(place_rows.shape)]
        + [whole(v.shape) for v in vectors]
        + [pl.BlockSpec(memory_space=pl.ANY)],
        out_specs=pl.BlockSpec((n, 128), lambda i: (0, lanes // 128 - 1)),
        out_shape=jax.ShapeDtypeStruct((n, lanes), BF16),
        input_output_aliases={5: 0},
        compiler_params=params(60 * 1024 * 1024),
        name="stamp",
    )(place_rows, *vectors, packed)


def qgrad_kernel(s_ref, norm_ref, wcol_ref, p0, p1, p2, p3, f0, f1, out_ref, w):
    t = pl.program_id(0)
    rows = out_ref.shape[0]

    @pl.when(t == 0)
    def _():
        for j in range(4):
            v = jnp.exp(s_ref[:, j * rows : (j + 1) * rows] - norm_ref[...])
            if j == 0:
                eye = iota((rows, rows), 0) == iota((rows, rows), 1)
                v = jnp.where(eye, v - 1.0, v)
            w[:, j * rows : (j + 1) * rows] = v.astype(BF16)

    fetched = jnp.where(t < PARTS, f0[...].astype(F32), f1[...].astype(F32))
    acc = wcol_ref[...] * fetched
    for j, p in enumerate((p0, p1, p2, p3)):
        acc += dot(w[:, j * rows : (j + 1) * rows], p[...])
    out_ref[...] = acc


def qgrad(s, norm, wcol, passages, fetched):
    rows, width = passages[0].shape
    tile = width // (2 * PARTS)
    col = pl.BlockSpec((rows, tile), lambda t: (0, t))
    low = pl.BlockSpec((rows, tile), lambda t: (0, jnp.minimum(t, PARTS - 1)))
    high = pl.BlockSpec((rows, tile), lambda t: (0, jnp.maximum(t - PARTS, 0)))
    return pl.pallas_call(
        qgrad_kernel,
        grid=(2 * PARTS,),
        in_specs=[whole(s.shape), whole((rows, 1)), whole((rows, 1))] + [col] * 4 + [low, high],
        out_specs=col,
        out_shape=jax.ShapeDtypeStruct((rows, width), F32),
        scratch_shapes=[pltpu.VMEM((rows, 4 * rows), BF16)],
        compiler_params=params(),
        cost_estimate=pl.CostEstimate(
            flops=8 * rows * rows * width,
            bytes_accessed=14 * rows * width,
            transcendentals=4 * rows * rows,
        ),
        name="qgrad",
    )(s, norm, wcol, *passages, *fetched)


def pgrad_kernel(scale, p_ref, q0, q1, q2, q3, n0, n1, n2, n3, out_ref, wt):
    t = pl.program_id(0)
    rows = p_ref.shape[0]
    tile = out_ref.shape[1]
    queries = (q0, q1, q2, q3)

    @pl.when(t == 0)
    def _():
        for j, (q, norm) in enumerate(zip(queries, (n0, n1, n2, n3))):
            w = jnp.exp(dot_t(p_ref[...], q[...]) * scale - norm[0:1, :])
            if j == 0:
                eye = iota((rows, rows), 0) == iota((rows, rows), 1)
                w = jnp.where(eye, w - 1.0, w)
            wt[:, j * rows : (j + 1) * rows] = w.astype(BF16)

    at = pl.ds(pl.multiple_of(t * tile, tile), tile)
    acc = jnp.zeros(out_ref.shape, F32)
    for j, q in enumerate(queries):
        acc += dot(wt[:, j * rows : (j + 1) * rows], q[:, at])
    out_ref[...] = acc


def pgrad(scale, p, queries, norms):
    rows, width = p.shape
    tile = width // 8
    full = whole((rows, width))
    return pl.pallas_call(
        functools.partial(pgrad_kernel, scale),
        grid=(8,),
        in_specs=[full] * 5 + [whole((8, rows))] * 4,
        out_specs=pl.BlockSpec((rows, tile), lambda t: (0, t)),
        out_shape=jax.ShapeDtypeStruct((rows, width), F32),
        scratch_shapes=[pltpu.VMEM((rows, 4 * rows), BF16)],
        compiler_params=params(SMALL_BYTES),
        cost_estimate=pl.CostEstimate(
            flops=16 * rows * rows * width,
            bytes_accessed=14 * rows * width,
            transcendentals=4 * rows * rows,
        ),
        name="pgrad",
    )(p, *queries, *norms)


def finish_kernel(
    mean, half_ref, own_ref, pair_ref, main_ref, extra_ref, note_ref, part_ref, out_ref, mean_ref
):
    rows, width = out_ref.shape
    n, part = extra_ref.shape
    here = lax.div(iota((1, n), 1), n // 2) == half_ref[0]
    codes = jnp.where(here, own_ref[...], pair_ref[...])
    row = iota((rows, n), 0)
    hit = one(codes[0:1, :] == row)
    weight = note_ref[:, 0:1].astype(F32)
    late = (extra_ref[...].astype(F32) * note_ref[:, 1:2].astype(F32)).astype(BF16)
    for q in range(width // part):
        at = slice(q * part, (q + 1) * part)
        terms = (main_ref[:, at].astype(F32) * weight).astype(BF16)
        k = pl.program_id(0) * (width // part) + q
        acc = part_ref[:, at] + dot(hit, terms)
        out_ref[:, at] = acc + dot(one(codes[1:2, :] == row + rows * k), late)

    @pl.when(pl.program_id(0) == 0)
    def _():
        lane = iota(note_ref.shape, 1)
        parts = jnp.where((lane >= 2) & (lane <= 4), note_ref[...].astype(F32), 0.0)
        total = jnp.sum(parts, axis=0, keepdims=True)
        mean_ref[...] = jnp.sum(total, axis=1, keepdims=True) * mean


def finish(mean, half, own_rows, pair_rows, got, partial_grad):
    rows, width = partial_grad.shape
    n = got.shape[0]
    part = width // PARTS
    steps = 2
    col = pl.BlockSpec((rows, width // steps), lambda t: (0, t))
    return pl.pallas_call(
        functools.partial(finish_kernel, mean),
        grid=(steps,),
        in_specs=[
            pl.BlockSpec(memory_space=pltpu.SMEM),
            whole((2, n)),
            whole((2, n)),
            pl.BlockSpec((n, width // steps), lambda t: (0, t)),
            pl.BlockSpec((n, part), lambda t: (0, PARTS)),
            pl.BlockSpec((n, 128), lambda t: (0, (PARTS + 1) * part // 128)),
            col,
        ],
        out_specs=[col, whole((1, 1))],
        out_shape=[
            jax.ShapeDtypeStruct((rows, width), F32),
            jax.ShapeDtypeStruct((1, 1), F32),
        ],
        compiler_params=params(),
        cost_estimate=pl.CostEstimate(
            flops=4 * n * rows * width, bytes_accessed=11 * rows * width, transcendentals=0
        ),
        name="finish",
    )(half, own_rows, pair_rows, got, got, got, partial_grad)


def shards(queries, passages, hard_owner, hard_row):
    rows, width = queries.shape
    n_dp = lax.axis_size("dp")
    n_blk = lax.axis_size("blk")
    scale = 2.0 / math.sqrt(width)
    core = lax.rem(lax.axis_index("blk"), 2).astype(jnp.int32)
    half = lax.rem(lax.axis_index("dp") // 4, 2).astype(jnp.int32)
    half = lax.rem(half + core, 2).reshape(1)
    n = n_dp * MAIN

    def permute(x, table):
        return lax.ppermute(x, "blk", table)

    def exchange(x, groups):
        return lax.all_to_all(x, ("dp", "blk"), 0, 0, axis_index_groups=groups, tiled=True)

    p_low = passages[:, : width // 2]
    later, _ = lax.optimization_barrier((passages, p_low))
    p_halves = [p_low, later[:, width // 2 :]]
    pair_halves = [permute(p, PAIR) for p in p_halves]
    p_core = permute(passages, CORE)

    owner = hard_owner[:, 0]
    row = hard_row[:, 0]
    hits = (owner[:, None] == jnp.arange(n_dp, dtype=jnp.int32)[None, :]).astype(BF16)
    index = jnp.arange(rows, dtype=jnp.int32)
    before = (index[:, None] > index[None, :]).astype(BF16)
    slot = jnp.sum(dot(before, hits) * hits.astype(F32), axis=1).astype(jnp.int32)
    place = position(owner)
    chunk = jnp.where(core == 1, n_dp - 1 - place, place) * MAIN
    place_main = jnp.where(slot < MAIN, chunk + slot, -1)
    place_extra = jnp.where(slot < MAIN, -2 * MAIN, chunk + slot - MAIN)
    place_rows = jnp.stack([place_main, place_extra], axis=0)
    place_cols = jnp.stack([place_main, place_extra], axis=1)
    at = jnp.arange(n, dtype=jnp.int32)
    quarter = at % MAIN // EXTRA
    match = at[:, None] == place_main[None, :]
    code_main = jnp.sum(jnp.where(match, row[None, :] + 1, 0), axis=1) - 1
    match = (at - EXTRA * quarter)[:, None] == place_extra[None, :]
    code_extra = jnp.sum(jnp.where(match, row[None, :] + 1, 0), axis=1)
    code_extra = jnp.where(code_extra > 0, code_extra - 1 + rows * quarter, -1)
    codes = jnp.concatenate([code_main.reshape(n_dp, MAIN), code_extra.reshape(n_dp, MAIN)], axis=1)
    packed = pack(place_rows, queries, n)
    asked, packed = lax.optimization_barrier((exchange(codes, NEIGHBOURS), packed))
    asked = asked.reshape(n_dp, 2, MAIN)
    asked_cols = asked.transpose(0, 2, 1).reshape(n, 2)
    asked_rows = asked.transpose(1, 0, 2).reshape(2, n)
    asked_pair = permute(asked_rows, PAIR)

    got = [
        exchange(serve(half, asked_cols, p, o), NEIGHBOURS) for p, o in zip(p_halves, pair_halves)
    ]

    cut = 3 * rows // 4
    q_first, _ = lax.optimization_barrier((queries[:cut], codes))
    q_pair_first = permute(q_first, PAIR)
    q_core = permute(queries, CORE)

    p_pair = jnp.concatenate(pair_halves, axis=1)
    p_diag = permute(p_pair, CORE)
    passage_blocks = (passages, p_core, p_pair, p_diag)
    s, stats = scores(scale, queries, passage_blocks)
    fetched0, first = unpack(got[0], place_cols, queries)
    fetched1, wcol, norm, vectors = soft(scale, got[1], place_cols, queries, first, stats)

    vectors = (vectors, permute(vectors, CORE), permute(vectors, PAIR), permute(vectors, DIAG))

    q_last, *_ = lax.optimization_barrier((queries[cut:], *vectors[1:]))
    q_pair_last = permute(q_last, PAIR)
    sent = stamp(place_rows, vectors, packed)
    q_pair_first, sent = lax.optimization_barrier((q_pair_first, sent))
    q_pair = jnp.concatenate([q_pair_first, q_pair_last], axis=0)
    q_diag = permute(q_pair, CORE)
    terms = exchange(sent, COLUMNS)

    query_gradient = qgrad(s, norm, wcol, passage_blocks, (fetched0, fetched1))
    partial_grad = pgrad(scale, passages, (queries, q_core, q_pair, q_diag), vectors)
    mean = 1.0 / (rows * n_blk * n_dp)
    passage_gradient, loss = finish(mean, half, asked_rows, asked_pair, terms, partial_grad)
    return query_gradient, passage_gradient, loss.reshape(())


def solution(mesh):
    spec = P(("dp", "blk"), None)
    return jax.shard_map(
        shards,
        mesh=mesh,
        in_specs=(spec,) * 4,
        out_specs=(spec, spec, P()),
        check_vma=False,
    )
```

time: 187 us -> 147 us (0.79)
  Pallas kernels: 77.6 us -> 52.7 us
  waiting for transfers between devices: 38.8 us -> 32.2 us
  starting transfers between devices: 47.5 us -> 42.2 us
  other arithmetic: 3.97 us -> 1.64 us
    pallas_call x9 -> x7, Pallas kernels: 47.9 us -> 25.8 us  [the longest x2 6.95 us: serve(): pl.pallas_call(serve_kernel, grid=(1,), in_specs=[pl.BlockSpec(memory_spa...]
    ppermute x14 -> x12, waiting for transfers between devices: 31.9 us -> 20.3 us  [permute(): return lax.ppermute(x, 'blk', table)]
    all_to_all x1 -> x0, starting transfers between devices: 9.94 us -> none  [shards(): terms = lax.all_to_all(sent, 'dp', 0, 0, tiled=True)]
    all_to_all x3 -> x4, starting transfers between devices: 28.3 us -> 35.7 us  [exchange(): lax.all_to_all(x, ('dp', 'blk'), 0, 0, axis_index_groups=groups, tiled=True)]
    all_to_all x3 -> x4, waiting for transfers between devices: 6.87 us -> 12 us  [exchange(): lax.all_to_all(x, ('dp', 'blk'), 0, 0, axis_index_groups=groups, tiled=True)]
    pallas_call x1, Pallas kernels: 12.2 us -> 9.25 us  [pgrad(): pl.pallas_call(functools.partial(pgrad_kernel, scale), grid=(8,), in_spec...]
    ppermute x14 -> x12, starting transfers between devices: 9.22 us -> 6.52 us  [permute(): return lax.ppermute(x, 'blk', table)]
    unnamed x30 -> x42, local copies, waits for them, and re-layouts: 5.82 us -> 7.16 us
  transfers between devices with their start and end apart: 18 -> 16, of which waited for: 4 -> 10; matrix products, arithmetic and copies ran while one was open for 6% -> 10% of each run, Pallas kernels for 41% -> 33%
where the time goes in v2:
time: 147 us; the launch traced here: 145 us
  Pallas kernels  52.7 us (36%)
  starting transfers between devices  42.2 us (29%)
  waiting for transfers between devices  32.2 us (22%)
  local copies, waits for them, and re-layouts  15.3 us (10%)
  other arithmetic  1.64 us (1%)
    all_to_all x4, starting transfers between devices, exchange(): lax.all_to_all(x, ('dp', 'blk'), 0, 0, axis_index_groups=groups, tiled=True)  35.7 us
    ppermute x12, waiting for transfers between devices, permute(): return lax.ppermute(x, 'blk', table)  20.3 us
    all_to_all x4, waiting for transfers between devices, exchange(): lax.all_to_all(x, ('dp', 'blk'), 0, 0, axis_index_groups=groups, tiled=True)  12 us
    pallas_call x1, Pallas kernels, qgrad(): pl.pallas_call(qgrad_kernel, grid=(2 * PARTS,), in_specs=[whole(s.shape),...  10.2 us
    pallas_call x1, Pallas kernels, pgrad(): pl.pallas_call(functools.partial(pgrad_kernel, scale), grid=(8,), in_spec...  9.25 us
    pallas_call x1, Pallas kernels, scores(): pl.pallas_call(functools.partial(scores_kernel, scale), grid=(1,), in_spe...  7.46 us
    unnamed x42, local copies, waits for them, and re-layouts  7.16 us
    pallas_call x2, Pallas kernels, serve(): pl.pallas_call(serve_kernel, grid=(1,), in_specs=[pl.BlockSpec(memory_spa...  6.95 us
  transfers between devices with their start and end apart: 16, of which 10 were waited for; matrix products, arithmetic and copies ran while one was open for 10% of the time, Pallas kernels for 33%

profile of v2, /device:TPU:4, one launch (start us, length us, event | category | flops | bytes accessed | tf_op | source)
XLA Modules:
  0.0 145.3 jit_solution(14335003069894645386)
XLA Ops:
  6.9 9.6 %all-to-all-start = ((s32[32,1,16]{2,1,0:T(1,128)}), s32[32,1,16]{2,1,0:T(1,128)S(1)}, u32[]{:S(2)}, u32[]{:S(2)}) async-start(s32[32,1,16]{2,1,0:T(1,128)} %bitcast.4), calls=%async_computation | async-start | bytes 32768 | tf_op jit(solution)/shard_map/all_to_all | solution.py:459
  17.1 4.9 %pack.1.packed_ref = bf16[256,5248]{1,0:T(8,128)(2,1)} custom-call(s32[2,256]{1,0:T(2,128)} %pad_add_fusion.1.place_ref, bf16[256,4096]{1,0:T(8,128)(2,1)} %q0.1), custom_call_target="tpu_custom_call" | custom-call | flops 1073741824 | bytes 5242880 | tf_op jit(solution)/shard_map/pack/pallas_call | solution.py:124
  24.3 4.0 %collective-permute-done.1.pair_ref = bf16[256,2048]{1,0:T(8,128)(2,1)S(1)} collective-permute-done((bf16[256,2048]{1,0:T(8,128)(2,1)S(1)}, bf16[256,2048]{1,0:T(8,128)(2,1)S(1)}, u32[]{:S(2)}, u32[]{:S(2)}) %collective-permute-start.1) | collective-permute-done | bytes 1048608 | tf_op jit(solution)/shard_map/ppermute | solution.py:456
  29.2 3.5 %serve.3 = bf16[256,2560]{1,0:T(8,128)(2,1)} custom-call(s32[1]{0:T(128)} %bitcast.half_ref, s32[256,2]{1,0:T(8,128)} %bitcast.45, bf16[256,2048]{1,0:T(8,128)(2,1)} %copy-done.15, bf16[256,2048]{1,0:T(8,128)(2,1)} %copy-done.14), custom_call_target="tpu_custom_call" | custom-call | flops 536870912 | bytes 3670016 | tf_op jit(solution)/shard_map/serve/pallas_call | solution.py:86
  32.7 9.6 %all-to-all-start.2 = ((bf16[32,8,2560]{2,1,0:T(8,128)(2,1)}), bf16[32,8,2560]{2,1,0:T(8,128)(2,1)S(1)}, u32[]{:S(2)}, u32[]{:S(2)}) async-start(bf16[32,8,2560]{2,1,0:T(8,128)(2,1)} %bitcast.44), calls=%async_computation.2 | async-start | bytes 2621440 | tf_op jit(solution)/shard_map/all_to_all | solution.py:459
  43.7 6.5 %collective-permute-done.2.pair_ref = bf16[256,2048]{1,0:T(8,128)(2,1)} collective-permute-done((bf16[256,2048]{1,0:T(8,128)(2,1)}, bf16[256,2048]{1,0:T(8,128)(2,1)}, u32[]{:S(2)}, u32[]{:S(2)}) %collective-permute-start.2) | collective-permute-done | bytes 1048608 | tf_op jit(solution)/shard_map/ppermute | solution.py:456
  54.3 3.5 %serve.2 = bf16[256,2560]{1,0:T(8,128)(2,1)} custom-call(s32[1]{0:T(128)} %bitcast.half_ref, s32[256,2]{1,0:T(8,128)} %bitcast.46, bf16[256,2048]{1,0:T(8,128)(2,1)} %slice.13.own_ref, bf16[256,2048]{1,0:T(8,128)(2,1)} %collective-permute-done.2.pair_ref), custom_call_target="tpu_custom_call" | custom-call | flops 536870912 | bytes 3670016 | tf_op jit(solution)/shard_map/serve/pallas_call | solution.py:86
  57.8 1.6 %all-to-all-done.2 = bf16[32,8,2560]{2,1,0:T(8,128)(2,1)S(1)} async-done(((bf16[32,8,2560]{2,1,0:T(8,128)(2,1)}), bf16[32,8,2560]{2,1,0:T(8,128)(2,1)S(1)}, u32[]{:S(2)}, u32[]{:S(2)}) %all-to-all-start.2) | async-done | bytes 1310752 | tf_op jit(solution)/shard_map/all_to_all | solution.py:459
  59.4 8.1 %all-to-all-start.1 = ((bf16[32,8,2560]{2,1,0:T(8,128)(2,1)}), bf16[32,8,2560]{2,1,0:T(8,128)(2,1)}, u32[]{:S(2)}, u32[]{:S(2)}) async-start(bf16[32,8,2560]{2,1,0:T(8,128)(2,1)} %bitcast.43), calls=%async_computation.1 | async-start | bytes 2621440 | tf_op jit(solution)/shard_map/all_to_all | solution.py:459
  68.3 3.5 %unpack.1 = (bf16[256,2048]{1,0:T(8,128)(2,1)}, f32[256,1]{1,0:T(8,128)}) custom-call(bf16[256,2560]{1,0:T(8,128)(2,1)} %bitcast.42, s32[256,2]{1,0:T(8,128)} %copy.44.place_ref, bf16[256,4096]{1,0:T(8,128)(2,1)} %q0.1), custom_call_target="tpu_custom_call" | custom-call | flops 536870912 | bytes 3670016 | tf_op jit(solution)/shard_map/unpack/pallas_call | solution.py:201
  71.8 7.5 %scores.1 = (f32[256,1024]{1,0:T(8,128)}, f32[256,128]{1,0:T(8,128)}) custom-call(bf16[256,4096]{1,0:T(8,128)(2,1)} %q0.1, bf16[256,4096]{1,0:T(8,128)(2,1)} %p_ref.1, bf16[256,4096]{1,0:T(8,128)(2,1)} %collective-permute-done.p1, bf16[256,4096]{1,0:T(8,128)(2,1)} %copy-done.12, bf16[256,4096]{1,0:T(8,128)(2,1)} %collective-permute-done.3.p3), custom_call_target="tpu_custom_call" | custom-call | flops 2147483648 | bytes 10485760 | tf_op jit(solution)/shard_map/scores/pallas_call | solution.py:161
  79.3 5.9 %all-to-all-done.1 = bf16[32,8,2560]{2,1,0:T(8,128)(2,1)} async-done(((bf16[32,8,2560]{2,1,0:T(8,128)(2,1)}), bf16[32,8,2560]{2,1,0:T(8,128)(2,1)}, u32[]{:S(2)}, u32[]{:S(2)}) %all-to-all-start.1) | async-done | bytes 1310752 | tf_op jit(solution)/shard_map/all_to_all | solution.py:459
  85.2 3.6 %soft.1 = (bf16[256,2048]{1,0:T(8,128)(2,1)}, f32[256,1]{1,0:T(8,128)}, f32[256,1]{1,0:T(8,128)}, f32[8,256]{1,0:T(8,128)}) custom-call(bf16[256,2560]{1,0:T(8,128)(2,1)} %bitcast.12.got_ref, s32[256,2]{1,0:T(8,128)} %copy.44.place_ref, bf16[256,4096]{1,0:T(8,128)(2,1)} %q0.1, f32[256,1]{1,0:T(8,128)} %get-tuple-element.23.first_ref, ...), custom_call_target="tpu_custom_call" | custom-call | flops 536870912 | bytes 3670016 | tf_op jit(solution)/shard_map/soft/pallas_call | solution.py:241
  88.8 1.8 %collective-permute-start.7 = (f32[8,256]{1,0:T(8,128)}, f32[8,256]{1,0:T(8,128)S(1)}, u32[]{:S(2)}, u32[]{:S(2)}) collective-permute-start(f32[8,256]{1,0:T(8,128)} %get-tuple-element.30.v0.n0), channel_id=1, source_target_pairs={{0,2},{1,3},{2,0},{3,1},{4,6},{5,7},{6,4},{7,5},{8,10},{9,11},{10,... | collective-permute-start | bytes 24584 | tf_op jit(solution)/shard_map/ppermute | solution.py:456
  90.8 1.9 %collective-permute-done.7.v2.n2 = f32[8,256]{1,0:T(8,128)S(1)} collective-permute-done((f32[8,256]{1,0:T(8,128)}, f32[8,256]{1,0:T(8,128)S(1)}, u32[]{:S(2)}, u32[]{:S(2)}) %collective-permute-start.7) | collective-permute-done | bytes 8224 | tf_op jit(solution)/shard_map/ppermute | solution.py:456
  94.5 1.5 %stamp.1 = bf16[256,5248]{1,0:T(8,128)(2,1)} custom-call(s32[2,256]{1,0:T(2,128)} %pad_add_fusion.1.place_ref, f32[8,256]{1,0:T(8,128)} %get-tuple-element.30.v0.n0, f32[8,256]{1,0:T(8,128)} %copy-done.6, f32[8,256]{1,0:T(8,128)} %copy-done.8, f32[8,256]{1,0:T(8,128)} %copy-done.10, bf16[256,5248]{1,0:T(8,128)(2,1)} %pack.1.packed_ref), custom_call_target="tpu_custom_call", output_to_operand_aliasing={{}: (5, {})} | custom-call | tf_op jit(solution)/shard_map/stamp/pallas_call | solution.py:288
  96.1 8.5 %all-to-all-start.3 = ((bf16[32,8,5248]{2,1,0:T(8,128)(2,1)}), bf16[32,8,5248]{2,1,0:T(8,128)(2,1)}, u32[]{:S(2)}, u32[]{:S(2)}) async-start(bf16[32,8,5248]{2,1,0:T(8,128)(2,1)} %bitcast.41), calls=%async_computation.3 | async-start | bytes 5373952 | tf_op jit(solution)/shard_map/all_to_all | solution.py:459
  104.6 2.7 %constant_dynamic-update-slice_fusion.3 = bf16[256,4096]{1,0:T(8,128)(2,1)} fusion(bf16[192,4096]{1,0:T(8,128)(2,1)} %collective-permute-done.5), kind=kLoop, calls=%fused_computation.27 | loop fusion | bytes 3145728
  110.2 10.2 %qgrad.1 = f32[256,4096]{1,0:T(8,128)} custom-call(f32[256,1024]{1,0:T(8,128)} %get-tuple-element.21.s_ref, f32[256,1]{1,0:T(8,128)} %get-tuple-element.25.norm_ref, f32[256,1]{1,0:T(8,128)} %get-tuple-element.26.wcol_ref, bf16[256,4096]{1,0:T(8,128)(2,1)} %p_ref.1, bf16[256,4096]{1,0:T(8,128)(2,1)} %collective-permute-done.p1, ...), custom_call_target="tpu_custom_call" | custom-call | flops 2147483648 | bytes 14680064 | tf_op jit(solution)/shard_map/qgrad/pallas_call | solution.py:328
  120.5 9.2 %pgrad.1.part_ref = f32[256,4096]{1,0:T(8,128)S(1)} custom-call(bf16[256,4096]{1,0:T(8,128)(2,1)S(1)} %copy-done.3, bf16[256,4096]{1,0:T(8,128)(2,1)S(1)} %copy-done.1, bf16[256,4096]{1,0:T(8,128)(2,1)} %collective-permute-done.9.q1, bf16[256,4096]{1,0:T(8,128)(2,1)} %constant_dynamic-update-slice_fusion.2.q2, bf16[256,4096]{1,0:T(8,128)(2,1)} %collective-permute-done.11.q3, ...), custom_call_target="tpu_custom_call" | custom-call | flops 4294967296 | bytes 14680064 | tf_op jit(solution)/shard_map/pgrad/pallas_call | solution.py:371
  129.8 2.0 %copy-done.4 = f32[256,4096]{1,0:T(8,128)} copy-done((f32[256,4096]{1,0:T(8,128)}, f32[256,4096]{1,0:T(8,128)S(1)}, u32[]{:S(2)}) %copy-start.4) | copy-done | bytes 4194328
  131.7 5.3 %collective-permute-done.4.pair_ref = s32[2,256]{1,0:T(2,128)S(1)} collective-permute-done((s32[2,256]{1,0:T(2,128)S(1)}, s32[2,256]{1,0:T(2,128)S(1)}, u32[]{:S(2)}, u32[]{:S(2)}) %collective-permute-start.4) | collective-permute-done | bytes 2080 | tf_op jit(solution)/shard_map/ppermute | solution.py:456
  137.0 3.0 %all-to-all-done.3 = bf16[32,8,5248]{2,1,0:T(8,128)(2,1)} async-done(((bf16[32,8,5248]{2,1,0:T(8,128)(2,1)}), bf16[32,8,5248]{2,1,0:T(8,128)(2,1)}, u32[]{:S(2)}, u32[]{:S(2)}) %all-to-all-start.3) | async-done | bytes 2687008 | tf_op jit(solution)/shard_map/all_to_all | solution.py:459
  140.0 5.2 %finish.1 = (f32[256,4096]{1,0:T(8,128)}, f32[1,1]{1,0:T(1,128)}) custom-call(s32[1]{0:T(128)} %bitcast.half_ref, s32[2,256]{1,0:T(2,128)} %copy-done.17, s32[2,256]{1,0:T(2,128)} %copy-done.18, bf16[256,5248]{1,0:T(8,128)(2,1)} %bitcast.18.main_ref.extra_ref.note_ref, bf16[256,5248]{1,0:T(8,128)(2,1)} %bitcast.18.main_ref.extra_ref.note_ref, ...), custom_call_target="tpu_custom_call" | custom-call | flops 1073741824 | bytes 11534336 | tf_op jit(solution)/shard_map/finish/pallas_call | solution.py:420
  (91 shorter events, 21.2 us)
Async XLA Ops:
  0.7 71.2 %collective-permute-start = (bf16[256,4096]{1,0:T(8,128)(2,1)}, bf16[256,4096]{1,0:T(8,128)(2,1)}, u32[]{:S(2)}, u32[]{:S(2)}) collective-permute-start(bf16[256,4096]{1,0:T(8,128)(2,1)} %p_ref.1), channel_id=1, source_target_pairs={{0,1},{1,0},{2,3},{3,2},{4,5},{5,4},{6,7},{7,6},{8,9},{9,8},{10,11... | collective-permute-start | bytes 6291464 | tf_op jit(solution)/shard_map/ppermute | solution.py:456
  2.2 19.8 %copy-start.15 = (bf16[256,2048]{1,0:T(8,128)(2,1)}, bf16[256,2048]{1,0:T(8,128)(2,1)S(1)}, u32[]{:S(2)}) copy-start(bf16[256,2048]{1,0:T(8,128)(2,1)S(1)} %slice.12.own_ref) | copy-start | bytes 3145732
  2.2 26.1 %collective-permute-start.1 = (bf16[256,2048]{1,0:T(8,128)(2,1)S(1)}, bf16[256,2048]{1,0:T(8,128)(2,1)S(1)}, u32[]{:S(2)}, u32[]{:S(2)}) collective-permute-start(bf16[256,2048]{1,0:T(8,128)(2,1)S(1)} %slice.12.own_ref), channel_id=1, source_target_pairs={{0,2},{1,3},{2,0},{3,1},{4,6},{5,7},{6,4},{7,5},{8,10},{9,11},{10,... | collective-permute-start | bytes 3145736 | tf_op jit(solution)/shard_map/ppermute | solution.py:456
  4.5 45.7 %collective-permute-start.2 = (bf16[256,2048]{1,0:T(8,128)(2,1)}, bf16[256,2048]{1,0:T(8,128)(2,1)}, u32[]{:S(2)}, u32[]{:S(2)}) collective-permute-start(bf16[256,2048]{1,0:T(8,128)(2,1)} %slice.13.own_ref), channel_id=1, source_target_pairs={{0,2},{1,3},{2,0},{3,1},{4,6},{5,7},{6,4},{7,5},{8,10},{9,11},{10,... | collective-permute-start | bytes 3145736 | tf_op jit(solution)/shard_map/ppermute | solution.py:456
  6.9 16.6 %all-to-all-start = ((s32[32,1,16]{2,1,0:T(1,128)}), s32[32,1,16]{2,1,0:T(1,128)S(1)}, u32[]{:S(2)}, u32[]{:S(2)}) async-start(s32[32,1,16]{2,1,0:T(1,128)} %bitcast.4), calls=%async_computation | async-start | bytes 32768 | tf_op jit(solution)/shard_map/all_to_all | solution.py:459
  32.7 26.7 %all-to-all-start.2 = ((bf16[32,8,2560]{2,1,0:T(8,128)(2,1)}), bf16[32,8,2560]{2,1,0:T(8,128)(2,1)S(1)}, u32[]{:S(2)}, u32[]{:S(2)}) async-start(bf16[32,8,2560]{2,1,0:T(8,128)(2,1)} %bitcast.44), calls=%async_computation.2 | async-start | bytes 2621440 | tf_op jit(solution)/shard_map/all_to_all | solution.py:459
  51.6 20.2 %collective-permute-start.3 = (bf16[256,4096]{1,0:T(8,128)(2,1)S(1)}, bf16[256,4096]{1,0:T(8,128)(2,1)}, u32[]{:S(2)}, u32[]{:S(2)}) collective-permute-start(bf16[256,4096]{1,0:T(8,128)(2,1)S(1)} %constant_dynamic-update-slice_fusion.p2), channel_id=1, source_target_pairs={{0,1},{1,0},{2,3},{3,2},{4,5},{5,4},{6,7},{7,6},{8,9},{9,8},{10,11... | collective-permute-start | bytes 6291464 | tf_op jit(solution)/shard_map/ppermute | solution.py:456
  53.1 43.0 %collective-permute-start.5 = (bf16[192,4096]{1,0:T(8,128)(2,1)}, bf16[192,4096]{1,0:T(8,128)(2,1)}, u32[]{:S(2)}, u32[]{:S(2)}) collective-permute-start(bf16[192,4096]{1,0:T(8,128)(2,1)} %slice.14), channel_id=1, source_target_pairs={{0,2},{1,3},{2,0},{3,1},{4,6},{5,7},{6,4},{7,5},{8,10},{9,11},{10,... | collective-permute-start | bytes 4718600 | tf_op jit(solution)/shard_map/ppermute | solution.py:456
  59.4 25.8 %all-to-all-start.1 = ((bf16[32,8,2560]{2,1,0:T(8,128)(2,1)}), bf16[32,8,2560]{2,1,0:T(8,128)(2,1)}, u32[]{:S(2)}, u32[]{:S(2)}) async-start(bf16[32,8,2560]{2,1,0:T(8,128)(2,1)} %bitcast.43), calls=%async_computation.1 | async-start | bytes 2621440 | tf_op jit(solution)/shard_map/all_to_all | solution.py:459
  79.3 11.4 %copy-start.1 = (bf16[256,4096]{1,0:T(8,128)(2,1)S(1)}, bf16[256,4096]{1,0:T(8,128)(2,1)}, u32[]{:S(2)}) copy-start(bf16[256,4096]{1,0:T(8,128)(2,1)} %q0.1) | copy-start | bytes 6291460
  88.8 1.9 %collective-permute-start.6 = (f32[8,256]{1,0:T(8,128)}, f32[8,256]{1,0:T(8,128)S(1)}, u32[]{:S(2)}, u32[]{:S(2)}) collective-permute-start(f32[8,256]{1,0:T(8,128)} %get-tuple-element.30.v0.n0), channel_id=1, source_target_pairs={{0,1},{1,0},{2,3},{3,2},{4,5},{5,4},{6,7},{7,6},{8,9},{9,8},{10,11... | collective-permute-start | bytes 24584 | tf_op jit(solution)/shard_map/ppermute | solution.py:456
  88.8 3.9 %collective-permute-start.7 = (f32[8,256]{1,0:T(8,128)}, f32[8,256]{1,0:T(8,128)S(1)}, u32[]{:S(2)}, u32[]{:S(2)}) collective-permute-start(f32[8,256]{1,0:T(8,128)} %get-tuple-element.30.v0.n0), channel_id=1, source_target_pairs={{0,2},{1,3},{2,0},{3,1},{4,6},{5,7},{6,4},{7,5},{8,10},{9,11},{10,... | collective-permute-start | bytes 24584 | tf_op jit(solution)/shard_map/ppermute | solution.py:456
  90.6 3.3 %collective-permute-start.8 = (f32[8,256]{1,0:T(8,128)}, f32[8,256]{1,0:T(8,128)S(1)}, u32[]{:S(2)}, u32[]{:S(2)}) collective-permute-start(f32[8,256]{1,0:T(8,128)} %get-tuple-element.30.v0.n0), channel_id=1, source_target_pairs={{0,3},{1,2},{2,1},{3,0},{4,7},{5,6},{6,5},{7,4},{8,11},{9,10},{10,... | collective-permute-start | bytes 24584 | tf_op jit(solution)/shard_map/ppermute | solution.py:456
  93.9 14.8 %collective-permute-start.10 = (bf16[64,4096]{1,0:T(8,128)(2,1)S(1)}, bf16[64,4096]{1,0:T(8,128)(2,1)S(1)}, u32[]{:S(2)}, u32[]{:S(2)}) collective-permute-start(bf16[64,4096]{1,0:T(8,128)(2,1)S(1)} %slice.15), channel_id=1, source_target_pairs={{0,2},{1,3},{2,0},{3,1},{4,6},{5,7},{6,4},{7,5},{8,10},{9,11},{10,... | collective-permute-start | bytes 1572872 | tf_op jit(solution)/shard_map/ppermute | solution.py:456
  94.5 25.9 %collective-permute-start.9 = (bf16[256,4096]{1,0:T(8,128)(2,1)S(1)}, bf16[256,4096]{1,0:T(8,128)(2,1)}, u32[]{:S(2)}, u32[]{:S(2)}) collective-permute-start(bf16[256,4096]{1,0:T(8,128)(2,1)S(1)} %copy-done.1), channel_id=1, source_target_pairs={{0,1},{1,0},{2,3},{3,2},{4,5},{5,4},{6,7},{7,6},{8,9},{9,8},{10,11... | collective-permute-start | bytes 6291464 | tf_op jit(solution)/shard_map/ppermute | solution.py:456
  96.1 44.0 %all-to-all-start.3 = ((bf16[32,8,5248]{2,1,0:T(8,128)(2,1)}), bf16[32,8,5248]{2,1,0:T(8,128)(2,1)}, u32[]{:S(2)}, u32[]{:S(2)}) async-start(bf16[32,8,5248]{2,1,0:T(8,128)(2,1)} %bitcast.41), calls=%async_computation.3 | async-start | bytes 5373952 | tf_op jit(solution)/shard_map/all_to_all | solution.py:459
  109.5 10.9 %collective-permute-start.11 = (bf16[256,4096]{1,0:T(8,128)(2,1)}, bf16[256,4096]{1,0:T(8,128)(2,1)}, u32[]{:S(2)}, u32[]{:S(2)}) collective-permute-start(bf16[256,4096]{1,0:T(8,128)(2,1)} %constant_dynamic-update-slice_fusion.2.q2), channel_id=1, source_target_pairs={{0,1},{1,0},{2,3},{3,2},{4,5},{5,4},{6,7},{7,6},{8,9},{9,8},{10,11... | collective-permute-start | bytes 6291464 | tf_op jit(solution)/shard_map/ppermute | solution.py:456
  109.7 10.8 %copy-start.17 = (s32[2,256]{1,0:T(2,128)}, s32[2,256]{1,0:T(2,128)S(1)}, u32[]{:S(2)}) copy-start(s32[2,256]{1,0:T(2,128)S(1)} %reshape.330.own_ref) | copy-start | bytes 6148
  109.7 27.3 %collective-permute-start.4 = (s32[2,256]{1,0:T(2,128)S(1)}, s32[2,256]{1,0:T(2,128)S(1)}, u32[]{:S(2)}, u32[]{:S(2)}) collective-permute-start(s32[2,256]{1,0:T(2,128)S(1)} %reshape.330.own_ref), channel_id=1, source_target_pairs={{0,2},{1,3},{2,0},{3,1},{4,6},{5,7},{6,4},{7,5},{8,10},{9,11},{10,... | collective-permute-start | bytes 6152 | tf_op jit(solution)/shard_map/ppermute | solution.py:456
  110.2 10.3 %copy-start.3 = (bf16[256,4096]{1,0:T(8,128)(2,1)S(1)}, bf16[256,4096]{1,0:T(8,128)(2,1)}, u32[]{:S(2)}) copy-start(bf16[256,4096]{1,0:T(8,128)(2,1)} %p_ref.1) | copy-start | bytes 6291460
  110.2 10.3 %copy-start.5 = (f32[8,256]{1,0:T(8,128)S(1)}, f32[8,256]{1,0:T(8,128)}, u32[]{:S(2)}) copy-start(f32[8,256]{1,0:T(8,128)} %get-tuple-element.30.v0.n0) | copy-start | bytes 24580
  110.2 10.3 %copy-start.7 = (f32[8,256]{1,0:T(8,128)S(1)}, f32[8,256]{1,0:T(8,128)}, u32[]{:S(2)}) copy-start(f32[8,256]{1,0:T(8,128)} %copy-done.6) | copy-start | bytes 24580
  110.2 10.3 %copy-start.9 = (f32[8,256]{1,0:T(8,128)S(1)}, f32[8,256]{1,0:T(8,128)}, u32[]{:S(2)}) copy-start(f32[8,256]{1,0:T(8,128)} %copy-done.8) | copy-start | bytes 24580
  110.2 10.3 %copy-start.11 = (f32[8,256]{1,0:T(8,128)S(1)}, f32[8,256]{1,0:T(8,128)}, u32[]{:S(2)}) copy-start(f32[8,256]{1,0:T(8,128)} %copy-done.10) | copy-start | bytes 24580
  (12 other events, 49.1 us)

commit v3 on v2

--- a/solution.py
+++ b/solution.py
@@ -90,7 +90,7 @@
         + [whole(codes.shape), whole(own.shape), whole(pair.shape)],
         out_specs=whole((n, lanes)),
         out_shape=jax.ShapeDtypeStruct((n, lanes), BF16),
-        compiler_params=params(),
+        compiler_params=params(SMALL_BYTES),
         cost_estimate=pl.CostEstimate(
             flops=4 * n * rows * width, bytes_accessed=7 * rows * width, transcendentals=0
         ),
@@ -485,18 +485,21 @@
     code_extra = jnp.where(code_extra > 0, code_extra - 1 + rows * quarter, -1)
     codes = jnp.concatenate([code_main.reshape(n_dp, MAIN), code_extra.reshape(n_dp, MAIN)], axis=1)
     packed = pack(place_rows, queries, n)
-    asked, packed = lax.optimization_barrier((exchange(codes, NEIGHBOURS), packed))
+    cut = 3 * rows // 4
+    q_first = queries[:cut]
+    asked, packed, q_first = lax.optimization_barrier(
+        (exchange(codes, NEIGHBOURS), packed, q_first)
+    )
     asked = asked.reshape(n_dp, 2, MAIN)
     asked_cols = asked.transpose(0, 2, 1).reshape(n, 2)
     asked_rows = asked.transpose(1, 0, 2).reshape(2, n)
     asked_pair = permute(asked_rows, PAIR)
 
-    got = [
-        exchange(serve(half, asked_cols, p, o), NEIGHBOURS) for p, o in zip(p_halves, pair_halves)
-    ]
-
-    cut = 3 * rows // 4
-    q_first, _ = lax.optimization_barrier((queries[:cut], codes))
+    served = serve(half, asked_cols, p_halves[0], pair_halves[0])
+    pair_high, _ = lax.optimization_barrier((pair_halves[1], served))
+    served = [served, serve(half, asked_cols, p_halves[1], pair_high)]
+    got = [exchange(x, NEIGHBOURS) for x in served]
+
     q_pair_first = permute(q_first, PAIR)
     q_core = permute(queries, CORE)
 

time: 147 us -> 147 us (level)
  waiting for transfers between devices: 32.2 us -> 35.8 us
  local copies, waits for them, and re-layouts: 15.3 us -> 13.4 us
    ppermute x12, waiting for transfers between devices: 20.3 us -> 22.5 us  [permute(): return lax.ppermute(x, 'blk', table)]
    unnamed x42 -> x36, local copies, waits for them, and re-layouts: 7.16 us -> 6.04 us
  transfers between devices with their start and end apart: 16 -> 16, of which waited for: 10 -> 10; matrix products, arithmetic and copies ran while one was open for 10% -> 9% of each run, Pallas kernels for 33% -> 32%
where the time goes in v3:
time: 147 us
  Pallas kernels  52.4 us (36%)
  starting transfers between devices  42 us (29%)
  waiting for transfers between devices  35.8 us (24%)
  local copies, waits for them, and re-layouts  13.4 us (9%)
  other arithmetic  1.63 us (1%)
    all_to_all x4, starting transfers between devices, exchange(): lax.all_to_all(x, ('dp', 'blk'), 0, 0, axis_index_groups=groups, tiled=True)  34.7 us
    ppermute x12, waiting for transfers between devices, permute(): return lax.ppermute(x, 'blk', table)  22.5 us
    all_to_all x4, waiting for transfers between devices, exchange(): lax.all_to_all(x, ('dp', 'blk'), 0, 0, axis_index_groups=groups, tiled=True)  13.4 us
    pallas_call x1, Pallas kernels, qgrad(): pl.pallas_call(qgrad_kernel, grid=(2 * PARTS,), in_specs=[whole(s.shape),...  10.2 us
    pallas_call x1, Pallas kernels, pgrad(): pl.pallas_call(functools.partial(pgrad_kernel, scale), grid=(8,), in_spec...  9.25 us
    pallas_call x1, Pallas kernels, scores(): pl.pallas_call(functools.partial(scores_kernel, scale), grid=(1,), in_spe...  7.45 us
    ppermute x12, starting transfers between devices, permute(): return lax.ppermute(x, 'blk', table)  7.3 us
    pallas_call x2, Pallas kernels, serve(): pl.pallas_call(serve_kernel, grid=(1,), in_specs=[pl.BlockSpec(memory_spa...  6.53 us
  transfers between devices with their start and end apart: 16, of which 10 were waited for; matrix products, arithmetic and copies ran while one was open for 9% of the time, Pallas kernels for 32%

profile of v3, /device:TPU:4, one launch (start us, length us, event | category | flops | bytes accessed | tf_op | source)
XLA Modules:
  0.0 146.5 jit_solution(4508795444547103184)
XLA Ops:
  0.8 2.4 %slice.12.own_ref = bf16[256,2048]{1,0:T(8,128)(2,1)} slice(bf16[256,4096]{1,0:T(8,128)(2,1)} %p_ref.1), slice={[0:256], [0:2048]} | slice | bytes 2097152 | tf_op jit(solution)/shard_map/slice | solution.py:461
  6.9 9.6 %all-to-all-start = ((s32[32,1,16]{2,1,0:T(1,128)}), s32[32,1,16]{2,1,0:T(1,128)S(1)}, u32[]{:S(2)}, u32[]{:S(2)}) async-start(s32[32,1,16]{2,1,0:T(1,128)} %bitcast.4), calls=%async_computation | async-start | bytes 32768 | tf_op jit(solution)/shard_map/all_to_all | solution.py:459
  17.1 5.0 %pack.1.packed_ref = bf16[256,5248]{1,0:T(8,128)(2,1)} custom-call(s32[2,256]{1,0:T(2,128)} %pad_add_fusion.1.place_ref, bf16[256,4096]{1,0:T(8,128)(2,1)} %q0.1), custom_call_target="tpu_custom_call" | custom-call | flops 1073741824 | bytes 5242880 | tf_op jit(solution)/shard_map/pack/pallas_call | solution.py:124
  23.7 5.8 %collective-permute-done.1.pair_ref = bf16[256,2048]{1,0:T(8,128)(2,1)} collective-permute-done((bf16[256,2048]{1,0:T(8,128)(2,1)}, bf16[256,2048]{1,0:T(8,128)(2,1)}, u32[]{:S(2)}, u32[]{:S(2)}) %collective-permute-start.1) | collective-permute-done | bytes 1048608 | tf_op jit(solution)/shard_map/ppermute | solution.py:456
  29.5 3.4 %serve.2 = bf16[256,2560]{1,0:T(8,128)(2,1)} custom-call(s32[1]{0:T(128)} %bitcast.half_ref, s32[256,2]{1,0:T(8,128)S(1)} %bitcast.41, bf16[256,2048]{1,0:T(8,128)(2,1)} %slice.12.own_ref, bf16[256,2048]{1,0:T(8,128)(2,1)} %collective-permute-done.1.pair_ref), custom_call_target="tpu_custom_call" | custom-call | flops 536870912 | bytes 3670016 | tf_op jit(solution)/shard_map/serve/pallas_call | solution.py:86
  32.9 9.6 %all-to-all-start.2 = ((bf16[32,8,2560]{2,1,0:T(8,128)(2,1)}), bf16[32,8,2560]{2,1,0:T(8,128)(2,1)}, u32[]{:S(2)}, u32[]{:S(2)}) async-start(bf16[32,8,2560]{2,1,0:T(8,128)(2,1)} %bitcast.14), calls=%async_computation.2 | async-start | bytes 2621440 | tf_op jit(solution)/shard_map/all_to_all | solution.py:459
  43.8 7.6 %collective-permute-done.2.pair_ref = bf16[256,2048]{1,0:T(8,128)(2,1)} collective-permute-done((bf16[256,2048]{1,0:T(8,128)(2,1)S(1)}, bf16[256,2048]{1,0:T(8,128)(2,1)}, u32[]{:S(2)}, u32[]{:S(2)}) %collective-permute-start.2) | collective-permute-done | bytes 1048608 | tf_op jit(solution)/shard_map/ppermute | solution.py:456
  54.1 3.1 %serve.3 = bf16[256,2560]{1,0:T(8,128)(2,1)} custom-call(s32[1]{0:T(128)} %bitcast.half_ref, s32[256,2]{1,0:T(8,128)S(1)} %bitcast.42, bf16[256,2048]{1,0:T(8,128)(2,1)S(1)} %slice.13.own_ref, bf16[256,2048]{1,0:T(8,128)(2,1)} %collective-permute-done.2.pair_ref), custom_call_target="tpu_custom_call" | custom-call | flops 536870912 | bytes 3670016 | tf_op jit(solution)/shard_map/serve/pallas_call | solution.py:86
  57.2 2.8 %all-to-all-done.2 = bf16[32,8,2560]{2,1,0:T(8,128)(2,1)} async-done(((bf16[32,8,2560]{2,1,0:T(8,128)(2,1)}), bf16[32,8,2560]{2,1,0:T(8,128)(2,1)}, u32[]{:S(2)}, u32[]{:S(2)}) %all-to-all-start.2) | async-done | bytes 1310752 | tf_op jit(solution)/shard_map/all_to_all | solution.py:459
  60.0 6.8 %all-to-all-start.1 = ((bf16[32,8,2560]{2,1,0:T(8,128)(2,1)}), bf16[32,8,2560]{2,1,0:T(8,128)(2,1)}, u32[]{:S(2)}, u32[]{:S(2)}) async-start(bf16[32,8,2560]{2,1,0:T(8,128)(2,1)} %bitcast.11), calls=%async_computation.1 | async-start | bytes 2621440 | tf_op jit(solution)/shard_map/all_to_all | solution.py:459
  67.7 3.5 %unpack.1 = (bf16[256,2048]{1,0:T(8,128)(2,1)}, f32[256,1]{1,0:T(8,128)}) custom-call(bf16[256,2560]{1,0:T(8,128)(2,1)} %bitcast.15.got_ref, s32[256,2]{1,0:T(8,128)} %copy.44.place_ref, bf16[256,4096]{1,0:T(8,128)(2,1)} %q0.1), custom_call_target="tpu_custom_call" | custom-call | flops 536870912 | bytes 3670016 | tf_op jit(solution)/shard_map/unpack/pallas_call | solution.py:201
  71.3 7.5 %scores.1 = (f32[256,1024]{1,0:T(8,128)}, f32[256,128]{1,0:T(8,128)}) custom-call(bf16[256,4096]{1,0:T(8,128)(2,1)} %q0.1, bf16[256,4096]{1,0:T(8,128)(2,1)} %p_ref.1, bf16[256,4096]{1,0:T(8,128)(2,1)} %collective-permute-done.p1, bf16[256,4096]{1,0:T(8,128)(2,1)} %copy-done.12, bf16[256,4096]{1,0:T(8,128)(2,1)} %collective-permute-done.3.p3), custom_call_target="tpu_custom_call" | custom-call | flops 2147483648 | bytes 10485760 | tf_op jit(solution)/shard_map/scores/pallas_call | solution.py:161
  78.7 6.0 %all-to-all-done.1 = bf16[32,8,2560]{2,1,0:T(8,128)(2,1)} async-done(((bf16[32,8,2560]{2,1,0:T(8,128)(2,1)}), bf16[32,8,2560]{2,1,0:T(8,128)(2,1)}, u32[]{:S(2)}, u32[]{:S(2)}) %all-to-all-start.1) | async-done | bytes 1310752 | tf_op jit(solution)/shard_map/all_to_all | solution.py:459
  84.7 3.6 %soft.1 = (bf16[256,2048]{1,0:T(8,128)(2,1)}, f32[256,1]{1,0:T(8,128)}, f32[256,1]{1,0:T(8,128)}, f32[8,256]{1,0:T(8,128)}) custom-call(bf16[256,2560]{1,0:T(8,128)(2,1)} %bitcast.12.got_ref, s32[256,2]{1,0:T(8,128)} %copy.44.place_ref, bf16[256,4096]{1,0:T(8,128)(2,1)} %q0.1, f32[256,1]{1,0:T(8,128)} %get-tuple-element.25.first_ref, ...), custom_call_target="tpu_custom_call" | custom-call | flops 536870912 | bytes 3670016 | tf_op jit(solution)/shard_map/soft/pallas_call | solution.py:241
  88.3 2.2 %collective-permute-start.7 = (f32[8,256]{1,0:T(8,128)}, f32[8,256]{1,0:T(8,128)S(1)}, u32[]{:S(2)}, u32[]{:S(2)}) collective-permute-start(f32[8,256]{1,0:T(8,128)} %get-tuple-element.32.v0.n0), channel_id=1, source_target_pairs={{0,2},{1,3},{2,0},{3,1},{4,6},{5,7},{6,4},{7,5},{8,10},{9,11},{10,... | collective-permute-start | bytes 24584 | tf_op jit(solution)/shard_map/ppermute | solution.py:456
  90.7 1.7 %collective-permute-done.7.v2.n2 = f32[8,256]{1,0:T(8,128)S(1)} collective-permute-done((f32[8,256]{1,0:T(8,128)}, f32[8,256]{1,0:T(8,128)S(1)}, u32[]{:S(2)}, u32[]{:S(2)}) %collective-permute-start.7) | collective-permute-done | bytes 8224 | tf_op jit(solution)/shard_map/ppermute | solution.py:456
  96.0 8.7 %all-to-all-start.3 = ((bf16[32,8,5248]{2,1,0:T(8,128)(2,1)}), bf16[32,8,5248]{2,1,0:T(8,128)(2,1)}, u32[]{:S(2)}, u32[]{:S(2)}) async-start(bf16[32,8,5248]{2,1,0:T(8,128)(2,1)} %bitcast.43), calls=%async_computation.3 | async-start | bytes 5373952 | tf_op jit(solution)/shard_map/all_to_all | solution.py:459
  104.7 2.7 %constant_dynamic-update-slice_fusion.3 = bf16[256,4096]{1,0:T(8,128)(2,1)} fusion(bf16[192,4096]{1,0:T(8,128)(2,1)} %collective-permute-done.5), kind=kLoop, calls=%fused_computation.27 | loop fusion | bytes 3145728
  110.2 10.2 %qgrad.1 = f32[256,4096]{1,0:T(8,128)} custom-call(f32[256,1024]{1,0:T(8,128)} %get-tuple-element.22.s_ref, f32[256,1]{1,0:T(8,128)} %get-tuple-element.27.norm_ref, f32[256,1]{1,0:T(8,128)} %get-tuple-element.28.wcol_ref, bf16[256,4096]{1,0:T(8,128)(2,1)} %p_ref.1, bf16[256,4096]{1,0:T(8,128)(2,1)} %collective-permute-done.p1, ...), custom_call_target="tpu_custom_call" | custom-call | flops 2147483648 | bytes 14680064 | tf_op jit(solution)/shard_map/qgrad/pallas_call | solution.py:328
  120.5 9.2 %pgrad.1.part_ref = f32[256,4096]{1,0:T(8,128)S(1)} custom-call(bf16[256,4096]{1,0:T(8,128)(2,1)S(1)} %copy-done.3, bf16[256,4096]{1,0:T(8,128)(2,1)S(1)} %copy-done.1, bf16[256,4096]{1,0:T(8,128)(2,1)} %collective-permute-done.9.q1, bf16[256,4096]{1,0:T(8,128)(2,1)} %constant_dynamic-update-slice_fusion.2.q2, bf16[256,4096]{1,0:T(8,128)(2,1)} %collective-permute-done.11.q3, ...), custom_call_target="tpu_custom_call" | custom-call | flops 4294967296 | bytes 14680064 | tf_op jit(solution)/shard_map/pgrad/pallas_call | solution.py:371
  129.8 2.0 %copy-done.4 = f32[256,4096]{1,0:T(8,128)} copy-done((f32[256,4096]{1,0:T(8,128)}, f32[256,4096]{1,0:T(8,128)S(1)}, u32[]{:S(2)}) %copy-start.4) | copy-done | bytes 4194328
  131.7 5.1 %collective-permute-done.4.pair_ref = s32[2,256]{1,0:T(2,128)S(1)} collective-permute-done((s32[2,256]{1,0:T(2,128)S(1)}, s32[2,256]{1,0:T(2,128)S(1)}, u32[]{:S(2)}, u32[]{:S(2)}) %collective-permute-start.4) | collective-permute-done | bytes 2080 | tf_op jit(solution)/shard_map/ppermute | solution.py:456
  136.8 4.5 %all-to-all-done.3 = bf16[32,8,5248]{2,1,0:T(8,128)(2,1)} async-done(((bf16[32,8,5248]{2,1,0:T(8,128)(2,1)}), bf16[32,8,5248]{2,1,0:T(8,128)(2,1)}, u32[]{:S(2)}, u32[]{:S(2)}) %all-to-all-start.3) | async-done | bytes 2687008 | tf_op jit(solution)/shard_map/all_to_all | solution.py:459
  141.3 5.3 %finish.1 = (f32[256,4096]{1,0:T(8,128)}, f32[1,1]{1,0:T(1,128)}) custom-call(s32[1]{0:T(128)} %bitcast.half_ref, s32[2,256]{1,0:T(2,128)} %copy-done.14, s32[2,256]{1,0:T(2,128)} %copy-done.15, bf16[256,5248]{1,0:T(8,128)(2,1)} %bitcast.18.main_ref.extra_ref.note_ref, bf16[256,5248]{1,0:T(8,128)(2,1)} %bitcast.18.main_ref.extra_ref.note_ref, ...), custom_call_target="tpu_custom_call" | custom-call | flops 1073741824 | bytes 11534336 | tf_op jit(solution)/shard_map/finish/pallas_call | solution.py:420
  (85 shorter events, 17.3 us)
Async XLA Ops:
  0.7 70.6 %collective-permute-start = (bf16[256,4096]{1,0:T(8,128)(2,1)}, bf16[256,4096]{1,0:T(8,128)(2,1)}, u32[]{:S(2)}, u32[]{:S(2)}) collective-permute-start(bf16[256,4096]{1,0:T(8,128)(2,1)} %p_ref.1), channel_id=1, source_target_pairs={{0,1},{1,0},{2,3},{3,2},{4,5},{5,4},{6,7},{7,6},{8,9},{9,8},{10,11... | collective-permute-start | bytes 6291464 | tf_op jit(solution)/shard_map/ppermute | solution.py:456
  3.2 26.3 %collective-permute-start.1 = (bf16[256,2048]{1,0:T(8,128)(2,1)}, bf16[256,2048]{1,0:T(8,128)(2,1)}, u32[]{:S(2)}, u32[]{:S(2)}) collective-permute-start(bf16[256,2048]{1,0:T(8,128)(2,1)} %slice.12.own_ref), channel_id=1, source_target_pairs={{0,2},{1,3},{2,0},{3,1},{4,6},{5,7},{6,4},{7,5},{8,10},{9,11},{10,... | collective-permute-start | bytes 3145736 | tf_op jit(solution)/shard_map/ppermute | solution.py:456
  4.5 46.9 %collective-permute-start.2 = (bf16[256,2048]{1,0:T(8,128)(2,1)S(1)}, bf16[256,2048]{1,0:T(8,128)(2,1)}, u32[]{:S(2)}, u32[]{:S(2)}) collective-permute-start(bf16[256,2048]{1,0:T(8,128)(2,1)S(1)} %slice.13.own_ref), channel_id=1, source_target_pairs={{0,2},{1,3},{2,0},{3,1},{4,6},{5,7},{6,4},{7,5},{8,10},{9,11},{10,... | collective-permute-start | bytes 3145736 | tf_op jit(solution)/shard_map/ppermute | solution.py:456
  6.9 16.6 %all-to-all-start = ((s32[32,1,16]{2,1,0:T(1,128)}), s32[32,1,16]{2,1,0:T(1,128)S(1)}, u32[]{:S(2)}, u32[]{:S(2)}) async-start(s32[32,1,16]{2,1,0:T(1,128)} %bitcast.4), calls=%async_computation | async-start | bytes 32768 | tf_op jit(solution)/shard_map/all_to_all | solution.py:459
  32.9 27.1 %all-to-all-start.2 = ((bf16[32,8,2560]{2,1,0:T(8,128)(2,1)}), bf16[32,8,2560]{2,1,0:T(8,128)(2,1)}, u32[]{:S(2)}, u32[]{:S(2)}) async-start(bf16[32,8,2560]{2,1,0:T(8,128)(2,1)} %bitcast.14), calls=%async_computation.2 | async-start | bytes 2621440 | tf_op jit(solution)/shard_map/all_to_all | solution.py:459
  52.7 7.3 %copy-start.12 = (bf16[256,4096]{1,0:T(8,128)(2,1)}, bf16[256,4096]{1,0:T(8,128)(2,1)S(1)}, u32[]{:S(2)}) copy-start(bf16[256,4096]{1,0:T(8,128)(2,1)S(1)} %constant_dynamic-update-slice_fusion.p2) | copy-start | bytes 6291460
  52.7 18.5 %collective-permute-start.3 = (bf16[256,4096]{1,0:T(8,128)(2,1)S(1)}, bf16[256,4096]{1,0:T(8,128)(2,1)}, u32[]{:S(2)}, u32[]{:S(2)}) collective-permute-start(bf16[256,4096]{1,0:T(8,128)(2,1)S(1)} %constant_dynamic-update-slice_fusion.p2), channel_id=1, source_target_pairs={{0,1},{1,0},{2,3},{3,2},{4,5},{5,4},{6,7},{7,6},{8,9},{9,8},{10,11... | collective-permute-start | bytes 6291464 | tf_op jit(solution)/shard_map/ppermute | solution.py:456
  52.8 43.2 %collective-permute-start.5 = (bf16[192,4096]{1,0:T(8,128)(2,1)}, bf16[192,4096]{1,0:T(8,128)(2,1)}, u32[]{:S(2)}, u32[]{:S(2)}) collective-permute-start(bf16[192,4096]{1,0:T(8,128)(2,1)} %slice.14), channel_id=1, source_target_pairs={{0,2},{1,3},{2,0},{3,1},{4,6},{5,7},{6,4},{7,5},{8,10},{9,11},{10,... | collective-permute-start | bytes 4718600 | tf_op jit(solution)/shard_map/ppermute | solution.py:456
  60.0 24.7 %all-to-all-start.1 = ((bf16[32,8,2560]{2,1,0:T(8,128)(2,1)}), bf16[32,8,2560]{2,1,0:T(8,128)(2,1)}, u32[]{:S(2)}, u32[]{:S(2)}) async-start(bf16[32,8,2560]{2,1,0:T(8,128)(2,1)} %bitcast.11), calls=%async_computation.1 | async-start | bytes 2621440 | tf_op jit(solution)/shard_map/all_to_all | solution.py:459
  78.7 11.9 %copy-start.1 = (bf16[256,4096]{1,0:T(8,128)(2,1)S(1)}, bf16[256,4096]{1,0:T(8,128)(2,1)}, u32[]{:S(2)}) copy-start(bf16[256,4096]{1,0:T(8,128)(2,1)} %q0.1) | copy-start | bytes 6291460
  88.3 2.3 %collective-permute-start.6 = (f32[8,256]{1,0:T(8,128)}, f32[8,256]{1,0:T(8,128)S(1)}, u32[]{:S(2)}, u32[]{:S(2)}) collective-permute-start(f32[8,256]{1,0:T(8,128)} %get-tuple-element.32.v0.n0), channel_id=1, source_target_pairs={{0,1},{1,0},{2,3},{3,2},{4,5},{5,4},{6,7},{7,6},{8,9},{9,8},{10,11... | collective-permute-start | bytes 24584 | tf_op jit(solution)/shard_map/ppermute | solution.py:456
  88.3 4.0 %collective-permute-start.7 = (f32[8,256]{1,0:T(8,128)}, f32[8,256]{1,0:T(8,128)S(1)}, u32[]{:S(2)}, u32[]{:S(2)}) collective-permute-start(f32[8,256]{1,0:T(8,128)} %get-tuple-element.32.v0.n0), channel_id=1, source_target_pairs={{0,2},{1,3},{2,0},{3,1},{4,6},{5,7},{6,4},{7,5},{8,10},{9,11},{10,... | collective-permute-start | bytes 24584 | tf_op jit(solution)/shard_map/ppermute | solution.py:456
  90.5 3.3 %collective-permute-start.8 = (f32[8,256]{1,0:T(8,128)}, f32[8,256]{1,0:T(8,128)S(1)}, u32[]{:S(2)}, u32[]{:S(2)}) collective-permute-start(f32[8,256]{1,0:T(8,128)} %get-tuple-element.32.v0.n0), channel_id=1, source_target_pairs={{0,3},{1,2},{2,1},{3,0},{4,7},{5,6},{6,5},{7,4},{8,11},{9,10},{10,... | collective-permute-start | bytes 24584 | tf_op jit(solution)/shard_map/ppermute | solution.py:456
  93.8 14.6 %collective-permute-start.10 = (bf16[64,4096]{1,0:T(8,128)(2,1)S(1)}, bf16[64,4096]{1,0:T(8,128)(2,1)S(1)}, u32[]{:S(2)}, u32[]{:S(2)}) collective-permute-start(bf16[64,4096]{1,0:T(8,128)(2,1)S(1)} %slice.15), channel_id=1, source_target_pairs={{0,2},{1,3},{2,0},{3,1},{4,6},{5,7},{6,4},{7,5},{8,10},{9,11},{10,... | collective-permute-start | bytes 1572872 | tf_op jit(solution)/shard_map/ppermute | solution.py:456
  94.5 26.0 %collective-permute-start.9 = (bf16[256,4096]{1,0:T(8,128)(2,1)S(1)}, bf16[256,4096]{1,0:T(8,128)(2,1)}, u32[]{:S(2)}, u32[]{:S(2)}) collective-permute-start(bf16[256,4096]{1,0:T(8,128)(2,1)S(1)} %copy-done.1), channel_id=1, source_target_pairs={{0,1},{1,0},{2,3},{3,2},{4,5},{5,4},{6,7},{7,6},{8,9},{9,8},{10,11... | collective-permute-start | bytes 6291464 | tf_op jit(solution)/shard_map/ppermute | solution.py:456
  96.0 45.2 %all-to-all-start.3 = ((bf16[32,8,5248]{2,1,0:T(8,128)(2,1)}), bf16[32,8,5248]{2,1,0:T(8,128)(2,1)}, u32[]{:S(2)}, u32[]{:S(2)}) async-start(bf16[32,8,5248]{2,1,0:T(8,128)(2,1)} %bitcast.43), calls=%async_computation.3 | async-start | bytes 5373952 | tf_op jit(solution)/shard_map/all_to_all | solution.py:459
  109.2 11.2 %collective-permute-start.11 = (bf16[256,4096]{1,0:T(8,128)(2,1)}, bf16[256,4096]{1,0:T(8,128)(2,1)}, u32[]{:S(2)}, u32[]{:S(2)}) collective-permute-start(bf16[256,4096]{1,0:T(8,128)(2,1)} %constant_dynamic-update-slice_fusion.2.q2), channel_id=1, source_target_pairs={{0,1},{1,0},{2,3},{3,2},{4,5},{5,4},{6,7},{7,6},{8,9},{9,8},{10,11... | collective-permute-start | bytes 6291464 | tf_op jit(solution)/shard_map/ppermute | solution.py:456
  109.4 11.0 %copy-start.14 = (s32[2,256]{1,0:T(2,128)}, s32[2,256]{1,0:T(2,128)S(1)}, u32[]{:S(2)}) copy-start(s32[2,256]{1,0:T(2,128)S(1)} %reshape.330.own_ref) | copy-start | bytes 6148
  109.4 27.4 %collective-permute-start.4 = (s32[2,256]{1,0:T(2,128)S(1)}, s32[2,256]{1,0:T(2,128)S(1)}, u32[]{:S(2)}, u32[]{:S(2)}) collective-permute-start(s32[2,256]{1,0:T(2,128)S(1)} %reshape.330.own_ref), channel_id=1, source_target_pairs={{0,2},{1,3},{2,0},{3,1},{4,6},{5,7},{6,4},{7,5},{8,10},{9,11},{10,... | collective-permute-start | bytes 6152 | tf_op jit(solution)/shard_map/ppermute | solution.py:456
  110.2 10.3 %copy-start.3 = (bf16[256,4096]{1,0:T(8,128)(2,1)S(1)}, bf16[256,4096]{1,0:T(8,128)(2,1)}, u32[]{:S(2)}) copy-start(bf16[256,4096]{1,0:T(8,128)(2,1)} %p_ref.1) | copy-start | bytes 6291460
  110.2 10.3 %copy-start.5 = (f32[8,256]{1,0:T(8,128)S(1)}, f32[8,256]{1,0:T(8,128)}, u32[]{:S(2)}) copy-start(f32[8,256]{1,0:T(8,128)} %get-tuple-element.32.v0.n0) | copy-start | bytes 24580
  110.2 10.3 %copy-start.7 = (f32[8,256]{1,0:T(8,128)S(1)}, f32[8,256]{1,0:T(8,128)}, u32[]{:S(2)}) copy-start(f32[8,256]{1,0:T(8,128)} %copy-done.6) | copy-start | bytes 24580
  110.2 10.3 %copy-start.9 = (f32[8,256]{1,0:T(8,128)S(1)}, f32[8,256]{1,0:T(8,128)}, u32[]{:S(2)}) copy-start(f32[8,256]{1,0:T(8,128)} %copy-done.8) | copy-start | bytes 24580
  110.2 10.3 %copy-start.11 = (f32[8,256]{1,0:T(8,128)S(1)}, f32[8,256]{1,0:T(8,128)}, u32[]{:S(2)}) copy-start(f32[8,256]{1,0:T(8,128)} %copy-done.10) | copy-start | bytes 24580
  (9 other events, 31.4 us)
